TPU v7x, 32 devices: a whole 2x2x4 slice. The times are simulated.
32 devices in a mesh: dp: 4 (over y, x), fsdp: 8 (over z, core).
Axes of the slice: x: 2, y: 2, z: 4, core: 2. Of those that a mesh axis runs over, the one named last changes fastest.
Arguments:
- tokens: bfloat16 [4096, 2048], P(('dp', 'fsdp')), may hold values from -6 to 6
- out_cotangent: bfloat16 [4096, 2048], P(('dp', 'fsdp')), may hold values from -6 to 6
- counts: int32 [4, 8], P('dp', 'fsdp'), may hold values from 64 to 128, as said below
- forget_gap: float32 [2048], replicated, may hold values from 4.8828126e-05 to 0.5
- mixer_weight: float32 [2048, 4, 2048], P(('dp', 'fsdp')), may hold values from -0.15909903 to 0.15909903
- expand_weight: float32 [2048, 2, 5632], P(('dp', 'fsdp')), may hold values from -0.15909903 to 0.15909903
- shrink_weight: float32 [5632, 2048], P(('dp', 'fsdp')), may hold values from -0.09594032 to 0.09594032
- norm_gains: float32 [3, 2048], replicated, may hold values from 0.5 to 1.5
- mixer_first: float32 [2048, 4, 2048], P(('dp', 'fsdp')), may hold values from -23.04 to 23.04
- mixer_second: float32 [2048, 4, 2048], P(('dp', 'fsdp')), may hold values from 0.458752 to 3.670016
- expand_first: float32 [2048, 2, 5632], P(('dp', 'fsdp')), may hold values from -23.04 to 23.04
- expand_second: float32 [2048, 2, 5632], P(('dp', 'fsdp')), may hold values from 0.458752 to 3.670016
- shrink_first: float32 [5632, 2048], P(('dp', 'fsdp')), may hold values from -23.04 to 23.04
- shrink_second: float32 [5632, 2048], P(('dp', 'fsdp')), may hold values from 0.458752 to 3.670016
- gains_first: float32 [3, 2048], replicated, may hold values from -16 to 16
- gains_second: float32 [3, 2048], replicated, may hold values from 0.65536 to 2.62144
Outputs:
- block_output: bfloat16 [4096, 2048], P(('dp', 'fsdp'))
- token_grad: bfloat16 [4096, 2048], P(('dp', 'fsdp'))
- mixer_grad: float32 [2048, 4, 2048], P(('dp', 'fsdp'))
- mixer_first_new: float32 [2048, 4, 2048], P(('dp', 'fsdp'))
- mixer_second_new: float32 [2048, 4, 2048], P(('dp', 'fsdp'))
- mixer_weight_new: float32 [2048, 4, 2048], P(('dp', 'fsdp'))
- expand_grad: float32 [2048, 2, 5632], P(('dp', 'fsdp'))
- expand_first_new: float32 [2048, 2, 5632], P(('dp', 'fsdp'))
- expand_second_new: float32 [2048, 2, 5632], P(('dp', 'fsdp'))
- expand_weight_new: float32 [2048, 2, 5632], P(('dp', 'fsdp'))
- shrink_grad: float32 [5632, 2048], P(('dp', 'fsdp'))
- shrink_first_new: float32 [5632, 2048], P(('dp', 'fsdp'))
- shrink_second_new: float32 [5632, 2048], P(('dp', 'fsdp'))
- shrink_weight_new: float32 [5632, 2048], P(('dp', 'fsdp'))
- gains_grad: float32 [3, 2048], replicated
- gains_first_new: float32 [3, 2048], replicated
- gains_second_new: float32 [3, 2048], replicated
- gains_new: float32 [3, 2048], replicated
- trust_norms: float32 [2, 10], replicated
Inputs may be any that keep to these rules, and one draw needn't show every extreme that they name: `counts`: every device holds at least 64 tokens; in one group, drawn from the seed, every device is full.
All inputs are finite; a program needn't handle non-finite values.
Results may differ from a plain program's by a relative error of at most 0.011.
Values may be sent and summed in bfloat16 or wider, within the bound.
No kernel may reach another device: no remote copies, remote signals or barrier semaphores. Data moves between devices by JAX's collectives and lax.ppermute only.
A program may use at most 576 MiB of HBM per device.

v0:
```python
import jax
import jax.numpy as jnp
from jax import lax
from jax.sharding import PartitionSpec as P

STEP = 10


norm_eps = 1e-06
beta_one = 0.9
beta_two = 0.999
adam_eps = 1e-06
decay_rate = 0.01
learn_rate = 0.3


def prefix(array, axis, combine, identity, reverse):
    peers, here = (lax.axis_size(axis), lax.axis_index(axis))
    everything = jax.tree.map(lambda part: lax.all_gather(part, axis), array)
    start = jax.tree.map(
        lambda part, zero: jnp.broadcast_to(jnp.asarray(zero, part.dtype), part.shape),
        array,
        identity,
    )

    def step(k, before):
        at = peers - 1 - k if reverse else k
        reached = at > here if reverse else at < here
        new = combine(before, jax.tree.map(lambda part: part[at], everything))
        return jax.tree.map(lambda a, b: jnp.where(reached, a, b), new, before)

    return lax.fori_loop(0, peers, step, start)


def rms_scale(values):
    return lax.rsqrt(jnp.mean(values * values, axis=-1, keepdims=True) + norm_eps)


def rms_back(upstream, normed, scale):
    return scale * (upstream - normed * jnp.mean(upstream * normed, axis=-1, keepdims=True))


def silu_slope(values):
    squashed = jax.nn.sigmoid(values)
    return squashed * (1.0 + values * (1.0 - squashed))


def link(first, second):
    return (first[0] * second[0], second[0] * first[1] + second[1])


def matrix_squares(mixer, expand, shrink):
    return jnp.concatenate(
        [
            jnp.sum(mixer * mixer, axis=(0, 2)),
            jnp.sum(expand * expand, axis=(0, 2)),
            jnp.sum(shrink * shrink)[None],
        ]
    )


def adam_direction(weight, grad, first, second):
    bias_one = 1.0 - beta_one**STEP
    bias_two = 1.0 - beta_two**STEP
    first_new = beta_one * first + (1.0 - beta_one) * grad
    second_new = beta_two * second + (1.0 - beta_two) * grad * grad
    update = (
        first_new / bias_one / (jnp.sqrt(second_new / bias_two) + adam_eps) + decay_rate * weight
    )
    return (first_new, second_new, update)


def apply_trust(weight, update, weight_sq, update_sq, shape):
    ratio = jnp.sqrt(weight_sq) / (jnp.sqrt(update_sq) + adam_eps)
    return weight - learn_rate * ratio.reshape(shape) * update


def body(
    tokens,
    out_cotangent,
    counts,
    forget_gap,
    mixer_weight,
    expand_weight,
    shrink_weight,
    norm_gains,
    mixer_first,
    mixer_second,
    expand_first,
    expand_second,
    shrink_first,
    shrink_second,
    gains_first,
    gains_second,
):
    f32 = jnp.float32
    bf16 = jnp.bfloat16
    rows_here = tokens.shape[0]
    valid_rows = (lax.iota(jnp.int32, rows_here) < counts[0, 0]).astype(f32)[:, None]
    mixer_full = lax.all_gather(mixer_weight.astype(bf16), ("dp", "fsdp"), axis=0, tiled=True)
    inputs = tokens.astype(f32)
    scale_one = rms_scale(inputs)
    normed_one = inputs * scale_one
    input_low = (normed_one * norm_gains[0]).astype(bf16)
    projected = jnp.einsum("td,dke->tke", input_low, mixer_full[:, :3], preferred_element_type=f32)
    in_logit = projected[:, 0]
    forget_logit = projected[:, 1]
    out_logit = projected[:, 2]
    squashed = jax.nn.sigmoid(forget_logit)
    intake = forget_gap * (1.0 - squashed) * valid_rows
    forget = 1.0 - intake
    in_silu = jax.nn.silu(in_logit)
    inflow = in_silu * intake
    running_prod, local_hidden = lax.associative_scan(link, (forget, inflow), axis=0)
    carried = prefix(
        (running_prod[-1], local_hidden[-1]),
        "fsdp",
        link,
        (jnp.ones_like(forget_gap), jnp.zeros_like(forget_gap)),
        False,
    )
    hidden_seq = local_hidden + running_prod * carried[1]
    hidden_prev = jnp.concatenate([carried[1][None], hidden_seq[:-1]], 0)
    scale_two = rms_scale(hidden_seq)
    normed_two = hidden_seq * scale_two
    out_swish = jax.nn.silu(out_logit)
    mix_low = (normed_two * norm_gains[1] * out_swish).astype(bf16)
    mixed = jnp.dot(mix_low, mixer_full[:, 3], preferred_element_type=f32)
    residual = inputs + mixed
    expand_full, shrink_full = (
        lax.all_gather(expand_weight.astype(bf16), ("dp", "fsdp"), axis=0, tiled=True),
        lax.all_gather(shrink_weight.astype(bf16), ("dp", "fsdp"), axis=0, tiled=True),
    )
    scale_three = rms_scale(residual)
    normed_three = residual * scale_three
    feed_low = (normed_three * norm_gains[2]).astype(bf16)
    expanded = jnp.einsum("td,dkf->tkf", feed_low, expand_full, preferred_element_type=f32)
    gate_silu = jax.nn.silu(expanded[:, 0])
    up_value = expanded[:, 1]
    product_low = (gate_silu * up_value).astype(bf16)
    result = (residual + jnp.dot(product_low, shrink_full, preferred_element_type=f32)) * valid_rows
    block_output = result.astype(bf16)
    mixer_back = lax.all_gather(mixer_weight.astype(bf16), ("dp", "fsdp"), axis=0, tiled=True)
    expand_back, shrink_back = (
        lax.all_gather(expand_weight.astype(bf16), ("dp", "fsdp"), axis=0, tiled=True),
        lax.all_gather(shrink_weight.astype(bf16), ("dp", "fsdp"), axis=0, tiled=True),
    )
    cotangent_low = (out_cotangent.astype(f32) * valid_rows).astype(bf16)
    grad_product = lax.dot_general(
        cotangent_low, shrink_back, (((1,), (1,)), ((), ())), preferred_element_type=f32
    )
    grad_gate = grad_product * up_value * silu_slope(expanded[:, 0])
    grad_up = grad_product * gate_silu
    grad_expanded = jnp.stack([grad_gate, grad_up], 1).astype(bf16)
    grad_feed = jnp.einsum("tkf,dkf->td", grad_expanded, expand_back, preferred_element_type=f32)
    gain_three = jnp.sum(grad_feed * normed_three, 0)
    grad_residual = cotangent_low.astype(f32) + rms_back(
        grad_feed * norm_gains[2], normed_three, scale_three
    )
    residual_low = grad_residual.astype(bf16)
    grad_mix = lax.dot_general(
        residual_low, mixer_back[:, 3], (((1,), (1,)), ((), ())), preferred_element_type=f32
    )
    gain_two = jnp.sum(grad_mix * normed_two * out_swish, 0)
    grad_out_logit = grad_mix * normed_two * norm_gains[1] * silu_slope(out_logit)
    grad_hidden = rms_back(grad_mix * norm_gains[1] * out_swish, normed_two, scale_two)
    forget_next = jnp.concatenate([forget[1:], jnp.ones_like(forget[:1])], 0)
    reverse_prod, reverse_local = lax.associative_scan(
        link, (forget_next[::-1], grad_hidden[::-1]), axis=0
    )
    reverse_prod = reverse_prod[::-1]
    reverse_local = reverse_local[::-1]
    incoming = prefix(
        (running_prod[-1], forget[0] * reverse_local[0]),
        "fsdp",
        link,
        (jnp.ones_like(forget_gap), jnp.zeros_like(forget_gap)),
        True,
    )
    adjoint = reverse_local + reverse_prod * incoming[1]
    grad_in_logit = adjoint * intake * silu_slope(in_logit)
    grad_forget_logit = (
        forget_gap
        * valid_rows
        * squashed
        * (1.0 - squashed)
        * (adjoint * hidden_prev - adjoint * in_silu)
    )
    grad_projected = jnp.stack([grad_in_logit, grad_forget_logit, grad_out_logit], 1).astype(bf16)
    grad_input = jnp.einsum(
        "tke,dke->td", grad_projected, mixer_back[:, :3], preferred_element_type=f32
    )
    gain_one = jnp.sum(grad_input * normed_one, 0)
    token_grad = (
        grad_residual + rms_back(grad_input * norm_gains[0], normed_one, scale_one)
    ).astype(bf16)
    shrink_grad = lax.psum_scatter(
        lax.dot_general(
            product_low, cotangent_low, (((0,), (0,)), ((), ())), preferred_element_type=f32
        ),
        ("dp", "fsdp"),
        scatter_dimension=0,
        tiled=True,
    )
    expand_grad = lax.psum_scatter(
        jnp.einsum("td,tkf->dkf", feed_low, grad_expanded, preferred_element_type=f32),
        ("dp", "fsdp"),
        scatter_dimension=0,
        tiled=True,
    )
    leading = jnp.einsum("td,tke->dke", input_low, grad_projected, preferred_element_type=f32)
    trailing = lax.dot_general(
        mix_low, residual_low, (((0,), (0,)), ((), ())), preferred_element_type=f32
    )
    mixer_grad = lax.psum_scatter(
        jnp.concatenate([leading, trailing[:, None]], 1),
        ("dp", "fsdp"),
        scatter_dimension=0,
        tiled=True,
    )
    gains_grad = lax.psum(jnp.stack([gain_one, gain_two, gain_three]), ("dp", "fsdp"))
    mixer_first_new, mixer_second_new, mixer_update = adam_direction(
        mixer_weight, mixer_grad, mixer_first, mixer_second
    )
    expand_first_new, expand_second_new, expand_update = adam_direction(
        expand_weight, expand_grad, expand_first, expand_second
    )
    shrink_first_new, shrink_second_new, shrink_update = adam_direction(
        shrink_weight, shrink_grad, shrink_first, shrink_second
    )
    gains_first_new, gains_second_new, gains_update = adam_direction(
        norm_gains, gains_grad, gains_first, gains_second
    )
    update_local = matrix_squares(mixer_update, expand_update, shrink_update)
    weight_sq, update_sq = lax.psum(
        (matrix_squares(mixer_weight, expand_weight, shrink_weight), update_local), ("dp", "fsdp")
    )
    mixer_weight_new = apply_trust(
        mixer_weight, mixer_update, weight_sq[0:4], update_sq[0:4], (1, 4, 1)
    )
    expand_weight_new = apply_trust(
        expand_weight, expand_update, weight_sq[4:6], update_sq[4:6], (1, 2, 1)
    )
    shrink_weight_new = apply_trust(
        shrink_weight, shrink_update, weight_sq[6], update_sq[6], (1, 1)
    )
    gain_weight_sq = jnp.sum(norm_gains * norm_gains, axis=1)
    gain_update_sq = jnp.sum(gains_update * gains_update, axis=1)
    gains_new = apply_trust(norm_gains, gains_update, gain_weight_sq, gain_update_sq, (3, 1))
    weight_norms = jnp.sqrt(jnp.concatenate([weight_sq, gain_weight_sq]))
    update_norms = jnp.sqrt(jnp.concatenate([update_sq, gain_update_sq]))
    trust_norms = jnp.stack([weight_norms, update_norms])
    return (
        block_output,
        token_grad,
        mixer_grad,
        mixer_first_new,
        mixer_second_new,
        mixer_weight_new,
        expand_grad,
        expand_first_new,
        expand_second_new,
        expand_weight_new,
        shrink_grad,
        shrink_first_new,
        shrink_second_new,
        shrink_weight_new,
        gains_grad,
        gains_first_new,
        gains_second_new,
        gains_new,
        trust_norms,
    )


def solution(mesh):
    return jax.shard_map(
        body,
        mesh=mesh,
        in_specs=(
            P(("dp", "fsdp"), None),
            P(("dp", "fsdp"), None),
            P("dp", "fsdp"),
            P(),
            P(("dp", "fsdp"), None, None),
            P(("dp", "fsdp"), None, None),
            P(("dp", "fsdp"), None),
            P(),
            P(("dp", "fsdp"), None, None),
            P(("dp", "fsdp"), None, None),
            P(("dp", "fsdp"), None, None),
            P(("dp", "fsdp"), None, None),
            P(("dp", "fsdp"), None),
            P(("dp", "fsdp"), None),
            P(),
            P(),
        ),
        out_specs=(
            P(("dp", "fsdp"), None),
            P(("dp", "fsdp"), None),
            P(("dp", "fsdp"), None, None),
            P(("dp", "fsdp"), None, None),
            P(("dp", "fsdp"), None, None),
            P(("dp", "fsdp"), None, None),
            P(("dp", "fsdp"), None, None),
            P(("dp", "fsdp"), None, None),
            P(("dp", "fsdp"), None, None),
            P(("dp", "fsdp"), None, None),
            P(("dp", "fsdp"), None),
            P(("dp", "fsdp"), None),
            P(("dp", "fsdp"), None),
            P(("dp", "fsdp"), None),
            P(),
            P(),
            P(),
            P(),
            P(),
        ),
        check_vma=False,
    )
```

profile of v0, /device:TPU:0, one launch (start us, length us, event | category | flops | bytes accessed | tf_op | source)
XLA Modules:
  0.0 2901.4 jit_solution(5561352195511804677)
XLA Ops:
  16.7 192.3 %all-gather.7.cloned.1.call-done = bf16[2048,4,2048]{2,0,1:T(8,128)(2,1)} async-done(((bf16[64,4,2048]{2,0,1:T(8,128)(2,1)}), bf16[2048,4,2048]{2,0,1:T(8,128)(2,1)}) %all-gather.7.cloned.1.call-update) | async-done | bytes 33554448 | tf_op jit(solution)/shard_map/all_gather | solution.py:100
  209.0 10.1 fusion.2
  292.8 14.1 all-gather
  318.9 14.0 all-gather.1
  344.2 122.2 %all-gather.9.cloned.1.call-done = bf16[2048,2,5632]{2,0,1:T(8,128)(2,1)} async-done(((bf16[64,2,5632]{2,0,1:T(8,128)(2,1)}), bf16[2048,2,5632]{2,0,1:T(8,128)(2,1)}) %all-gather.9.cloned.1.call-update) | async-done | bytes 46137360 | tf_op jit(solution)/shard_map/all_gather | solution.py:131
  466.4 20.7 fusion.66
  487.1 125.6 %all-gather.11.cloned.1.call-done = bf16[5632,2048]{1,0:T(8,128)(2,1)} async-done(((bf16[176,2048]{1,0:T(8,128)(2,1)}), bf16[5632,2048]{1,0:T(8,128)(2,1)}) %all-gather.11.cloned.1.call-update) | async-done | bytes 23068688 | tf_op jit(solution)/shard_map/all_gather | solution.py:132
  612.7 15.5 fusion.24
  628.2 19.3 fusion.84
  658.7 8.3 slice.570
  667.0 8.3 slice.579
  675.2 8.3 slice.572
  683.5 22.8 multiply_reduce_fusion.6
  723.6 8.3 slice.576
  731.8 8.3 slice.574
  836.8 8.3 slice.624
  868.3 8.9 rev.8
  890.9 8.9 rev.9
  900.7 14.8 all-gather.2
  915.5 9.5 convolution_bitcast_fusion
  925.0 7.3 while.31
  936.6 21.4 fusion.44
  957.9 43.9 %pad_maximum_fusion = f32[2048,4,2048]{2,0,1:T(8,128)} fusion(f32[2048,1,2048]{2,0,1:T(8,128)} %convolution_bitcast_fusion, f32[2048,3,2048]{2,0,1:T(8,128)} %fusion.44), kind=kLoop, calls=%fused_computation.6 | loop fusion | flops 16777216 | bytes 134217728 | tf_op jit(solution)/shard_map/concatenate | solution.py:216
  1003.2 34.0 %fusion.17 = f32[2048,2,5632]{2,0,1:T(8,128)} fusion(bf16[128,1,5632]{2,0,1:T(8,128)(2,1)} %get-tuple-element.373, bf16[128,1,5632]{2,0,1:T(8,128)(2,1)S(1)} %copy-done.14, f32[128,2048]{1,0:T(8,128)S(1)} %get-tuple-element.446, f32[2048]{0:T(1024)S(1)} %bitcast.150, f32[128]{0:T(128)S(1)} %copy-done.47), kind=kOutput, calls=%fused_computation.49 | convolution fusion | flops 5912133632 | bytes 96215552 | tf_op jit(solution)/shard_map/td,tkf->dkf/dot_general | solution.py:206
  1043.3 14.9 fusion.31
  1061.1 11.9 fusion.14
  1073.1 65.1 %reduce-scatter.8.cloned.1.call-done = f32[176,2048]{1,0:T(8,128)} async-done(((f32[5632,2048]{1,0:T(8,128)}), f32[176,2048]{1,0:T(8,128)}) %reduce-scatter.8.cloned.1.call-update) | async-done | bytes 1441808 | tf_op jit(solution)/shard_map/reduce_scatter | solution.py:197
  1145.0 701.3 %reduce-scatter.4.cloned.1.call-done = f32[64,4,2048]{2,0,1:T(8,128)} async-done(((f32[2048,4,2048]{2,0,1:T(8,128)}), f32[64,4,2048]{2,0,1:T(8,128)}) %reduce-scatter.4.cloned.1.call-update) | async-done | bytes 2097168 | tf_op jit(solution)/shard_map/reduce_scatter | solution.py:215
  1846.3 10.7 multiply_reduce_fusion.2
  1862.6 953.3 %reduce-scatter.6.cloned.1.call-done = f32[64,2,5632]{2,0,1:T(8,128)} async-done(((f32[2048,2,5632]{2,0,1:T(8,128)}), f32[64,2,5632]{2,0,1:T(8,128)}) %reduce-scatter.6.cloned.1.call-update) | async-done | bytes 2883600 | tf_op jit(solution)/shard_map/reduce_scatter | solution.py:205
  2815.9 8.6 multiply_reduce_fusion
  2827.9 37.2 %all-reduce.58 = (f32[7]{0:T(128)S(1)}, f32[7]{0:T(128)S(1)}, f32[3,2048]{1,0:T(4,128)S(1)}) all-reduce(f32[7]{0:T(128)S(1)} %pad_maximum_fusion.33, f32[7]{0:T(128)S(1)} %pad_maximum_fusion.32, f32[3,2048]{1,0:T(4,128)S(1)} %pad_maximum_fusion.26), channel_id=1, replica_groups=mesh['dp'=4,'fsdp'=8] {'dp','fsdp'}, use_global_device_ids=true, to_apply=%region_20.21 | all-reduce | flops 6158 | bytes 49264 | tf_op jit(solution)/shard_map/psum | solution.py:235
  (458 shorter events, 333.0 us)
Async XLA Ops:
  7.2 201.8 %all-gather.7.cloned.1.call-start = ((), (), s32[]{:S(2)}) async-start(), calls=%async_computation.3 | async-start | bytes 34603008 | tf_op jit(solution)/shard_map/all_gather | solution.py:100
  11.1 455.3 %all-gather.9.cloned.1.call-start = ((), (), s32[]{:S(2)}) async-start(), calls=%async_computation.4 | async-start | bytes 47579136 | tf_op jit(solution)/shard_map/all_gather | solution.py:131
  12.7 600.0 %all-gather.11.cloned.1.call-start = ((), (), s32[]{:S(2)}) async-start(), calls=%async_computation.5 | async-start | bytes 23789568 | tf_op jit(solution)/shard_map/all_gather | solution.py:132
  15.2 1123.0 %reduce-scatter.8.cloned.1.call-start = ((), (), s32[]{:S(2)}) async-start(), calls=%async_computation.8 | async-start | bytes 47579136 | tf_op jit(solution)/shard_map/reduce_scatter | solution.py:197
  15.9 203.2 %copy-start.67 = (f32[128]{0:T(128)}, f32[128]{0:T(128)S(1)}, u32[]{:S(2)}) copy-start(f32[128]{0:T(128)S(1)} %compare_convert_fusion) | copy-start | bytes 1540
  16.1 203.0 %copy-start.71 = (f32[128]{0:T(128)}, f32[128]{0:T(128)S(1)}, u32[]{:S(2)}) copy-start(f32[128]{0:T(128)S(1)} %add_rsqrt_fusion.2) | copy-start | bytes 1540
  16.7 192.3 %copy-start.43 = (f32[1,2048]{1,0:T(1,128)}, f32[1,2048]{1,0:T(1,128)S(1)}, u32[]{:S(2)}) copy-start(f32[1,2048]{1,0:T(1,128)S(1)} %get-tuple-element.424) | copy-start | bytes 24580
  209.0 11.8 copy-start.48
  273.2 9.0 copy-start.40
  275.3 7.5 copy-start.63
  291.6 19.9 copy-start.51
  291.8 41.8 %copy-start.25 = (f32[128,2048]{1,0:T(8,128)}, f32[128,2048]{1,0:T(8,128)S(1)}, u32[]{:S(2)}) copy-start(f32[128,2048]{1,0:T(8,128)S(1)} %pad.200) | copy-start | bytes 3145732
  291.8 41.8 %copy-start.24 = (f32[128,2048]{1,0:T(8,128)S(1)}, f32[128,2048]{1,0:T(8,128)}, u32[]{:S(2)}) copy-start(f32[128,2048]{1,0:T(8,128)} %pad.201) | copy-start | bytes 3145732
  344.1 657.9 %copy-start.2 = (f32[128,2048]{1,0:T(8,128)}, f32[128,2048]{1,0:T(8,128)S(1)}, u32[]{:S(2)}) copy-start(f32[128,2048]{1,0:T(8,128)S(1)} %get-tuple-element.446) | copy-start | bytes 3145732
  344.2 362.1 %copy-start.46 = (f32[128]{0:T(128)}, f32[128]{0:T(128)S(1)}, u32[]{:S(2)}) copy-start(f32[128]{0:T(128)S(1)} %add_rsqrt_fusion) | copy-start | bytes 1540
  466.4 146.3 %copy-start.68 = (f32[128]{0:T(128)S(1)}, f32[128]{0:T(128)}, u32[]{:S(2)}) copy-start(f32[128]{0:T(128)} %copy-done.67) | copy-start | bytes 1540
  647.4 1198.9 %reduce-scatter.4.cloned.1.call-start = ((), (), s32[]{:S(2)}) async-start(), calls=%async_computation.6 | async-start | bytes 69206016 | tf_op jit(solution)/shard_map/reduce_scatter | solution.py:215
  789.0 15.1 copy-start.39
  789.0 15.1 copy-start.42
  831.3 16.4 copy-start.55
  915.5 9.5 copy-start.34
  915.5 16.8 copy-start.49
  915.5 16.8 copy-start.69
  936.5 21.4 copy-start.27
  1001.8 1814.1 %reduce-scatter.6.cloned.1.call-start = ((), (), s32[]{:S(2)}) async-start(), calls=%async_computation.7 | async-start | bytes 95158272 | tf_op jit(solution)/shard_map/reduce_scatter | solution.py:205
  1043.3 15.0 copy-start.50
  1043.3 15.0 copy-start.70
  2815.9 9.4 copy-start.13
  2865.1 21.1 copy-start.60
  2880.9 7.6 copy-start.4
  2881.0 7.6 copy-start.15
  2881.0 7.6 copy-start.16
  (47 other events, 187.5 us)
Sparse Core Ops, SparseCore 0:
  11.7 197.3 all-gather.6
  212.6 253.8 all-gather.8
  469.9 142.7 all-gather.10
  647.6 490.5 reduce-scatter.7
  1140.4 705.8 reduce-scatter.3
  1848.6 967.3 reduce-scatter.5
where the time goes:
time: 2920 us; the launch traced here: 2900 us
  waiting for transfers between devices  2160 us (74%)
  local copies, waits for them, and re-layouts  284 us (10%)
  matrix products  192 us (7%)
  other arithmetic  166 us (6%)
  blocking collectives  80 us (3%)
    reduce_scatter x1, waiting for transfers between devices, body(): lax.psum_scatter(jnp.einsum('td,tkf->dkf', feed_low, grad_expanded, prefe...  953 us
    reduce_scatter x1, waiting for transfers between devices, body(): lax.psum_scatter(jnp.concatenate([leading, trailing[:, None]], 1), ('dp',...  701 us
    all_gather x1, waiting for transfers between devices, body(): lax.all_gather(mixer_weight.astype(bf16), ('dp', 'fsdp'), axis=0, tiled=T...  192 us
    all_gather x1, waiting for transfers between devices, body(): lax.all_gather(shrink_weight.astype(bf16), ('dp', 'fsdp'), axis=0, tiled=...  126 us
    all_gather x1, waiting for transfers between devices, body(): lax.all_gather(expand_weight.astype(bf16), ('dp', 'fsdp'), axis=0, tiled=...  122 us
    slice x49, local copies, waits for them, and re-layouts, body(): lax.associative_scan(link, (forget_next[::-1], grad_hidden[::-1]), axis=0)  119 us
    reduce_scatter x1, waiting for transfers between devices, body(): lax.psum_scatter(lax.dot_general(product_low, cotangent_low, (((0,), (0,)...  65.1 us
  transfers between devices with their start and end apart: 6, of which 6 were waited for; matrix products, arithmetic and copies ran while one was open for 19% of the time, Pallas kernels for 0%

commit v1 on v0

v1 whole, which is shorter than its diff:
```python
import functools

import jax
import jax.numpy as jnp
from jax import lax
from jax.experimental import pallas as pl
from jax.experimental.pallas import tpu as pltpu
from jax.sharding import PartitionSpec as P

STEP = 10


norm_eps = 1e-06
beta_one = 0.9
beta_two = 0.999
adam_eps = 1e-06
decay_rate = 0.01
learn_rate = 0.3

f32 = jnp.float32
bf16 = jnp.bfloat16

EXTRA = 128
TILE = 8
WIDE = 32
CHUNK = 64
VMEM_BYTES = 48 * 1024 * 1024


def rms_scale(values):
    return lax.rsqrt(jnp.mean(values * values, axis=-1, keepdims=True) + norm_eps)


def rms_back(upstream, normed, scale):
    return scale * (upstream - normed * jnp.mean(upstream * normed, axis=-1, keepdims=True))


def silu_slope(values):
    squashed = jax.nn.sigmoid(values)
    return squashed * (1.0 + values * (1.0 - squashed))


def squares_of(matrices):
    return jnp.sum(matrices * matrices, axis=(0, 2))


def adam_direction(weight, grad, first, second):
    bias_one = 1.0 - beta_one**STEP
    bias_two = 1.0 - beta_two**STEP
    first_new = beta_one * first + (1.0 - beta_one) * grad
    second_new = beta_two * second + (1.0 - beta_two) * grad * grad
    update = (
        first_new / bias_one / (jnp.sqrt(second_new / bias_two) + adam_eps) + decay_rate * weight
    )
    return (first_new, second_new, update)


def apply_trust(weight, update, weight_sq, update_sq, shape):
    ratio = jnp.sqrt(weight_sq) / (jnp.sqrt(update_sq) + adam_eps)
    return weight - learn_rate * ratio.reshape(shape) * update


def split_low(column):
    head = lax.reduce_precision(column, 8, 7)
    return jnp.concatenate([head, column - head], axis=1).astype(bf16)


def pad_columns(columns):
    return jnp.pad(columns, ((0, 0), (0, EXTRA - columns.shape[1])))


def tile_scan(decay, inflow, reverse):
    rows = decay.shape[0]
    place = lax.broadcasted_iota(jnp.int32, decay.shape, 0)
    shift = 1
    while shift < rows:
        amount = rows - shift if reverse else shift
        reached = place < rows - shift if reverse else place >= shift
        earlier_decay = jnp.where(reached, pltpu.roll(decay, amount, 0), 1.0)
        earlier_inflow = jnp.where(reached, pltpu.roll(inflow, amount, 0), 0.0)
        inflow = inflow + decay * earlier_inflow
        decay = decay * earlier_decay
        shift *= 2
    return decay, inflow


def by_chunks(rows, work):
    def step(i, nothing):
        work(pl.ds(pl.multiple_of(i * CHUNK, CHUNK), CHUNK))
        return nothing

    lax.fori_loop(0, rows // CHUNK, step, 0)


def tile_row(i, tile, core, slots, groups):
    block = lax.div(i, slots // tile)
    first = lax.rem(block + core, 2) * groups * slots
    return first + lax.rem(i, slots // tile) * tile


def tile_at(first, b, tile, slots):
    return pl.ds(pl.multiple_of(first + b * slots, tile), tile)


def recur_forward_kernel(
    core_ref, logits_ref, valid_ref, gap_ref, decay_ref, local_ref, ends_ref
):
    rows, width = local_ref.shape
    groups = ends_ref.shape[0] // 2
    slots = rows // (2 * groups)

    def gates(at):
        in_logit = logits_ref[at, pl.ds(0, width)]
        closed = 1.0 - jax.nn.sigmoid(logits_ref[at, pl.ds(width, width)])
        intake = gap_ref[...] * closed * valid_ref[at, :]
        decay_ref[at, :] = 1.0 - intake
        local_ref[at, :] = in_logit * jax.nn.sigmoid(in_logit) * intake

    by_chunks(rows, gates)

    def step(i, carried):
        first = tile_row(i, TILE, core_ref[0], slots, groups)
        after_tile = []
        for b, (carry_decay, carry) in enumerate(carried):
            at = tile_at(first, b, TILE, slots)
            decay, local = tile_scan(decay_ref[at, :], local_ref[at, :], False)
            hidden = local + decay * carry
            decay = decay * carry_decay
            decay_ref[at, :] = decay
            local_ref[at, :] = hidden
            after_tile.append((decay[TILE - 1 :, :], hidden[TILE - 1 :, :]))
        return tuple(after_tile)

    start = (jnp.ones((1, width), f32), jnp.zeros((1, width), f32))
    ends = lax.fori_loop(0, 2 * slots // TILE, step, (start,) * groups)
    ends_ref[...] = jnp.concatenate([end[0] for end in ends] + [end[1] for end in ends], axis=0)


def recur_mix_kernel(
    core_ref,
    logits_ref,
    decay_ref,
    local_ref,
    carry_ref,
    gain_ref,
    hidden_ref,
    before_ref,
    mix_ref,
    squares_ref,
):
    rows, width = local_ref.shape
    groups = carry_ref.shape[0]
    slots = rows // (2 * groups)

    def step(i, carried):
        first = tile_row(i, WIDE, core_ref[0], slots, groups)
        after_tile = []
        for b in range(groups):
            at = tile_at(first, b, WIDE, slots)
            hidden = local_ref[at, :] + decay_ref[at, :] * carry_ref[b : b + 1, :]
            place = lax.broadcasted_iota(jnp.int32, hidden.shape, 0)
            out_logit = logits_ref[at, pl.ds(2 * width, width)]
            swish = out_logit * jax.nn.sigmoid(out_logit)
            hidden_ref[at, :] = hidden
            before_ref[at, :] = jnp.where(place > 0, pltpu.roll(hidden, 1, 0), carried[b])
            squares_ref[at, :] = jnp.sum(hidden * hidden, axis=1, keepdims=True)
            mix_ref[at, :] = (hidden * gain_ref[...] * swish).astype(bf16)
            after_tile.append(hidden[WIDE - 1 :, :])
        return tuple(after_tile)

    start = tuple(carry_ref[b : b + 1, :] for b in range(groups))
    lax.fori_loop(0, 2 * slots // WIDE, step, start)


def recur_reverse_kernel(
    core_ref,
    logits_ref,
    hidden_ref,
    grad_mix_ref,
    valid_ref,
    scale_ref,
    mean_ref,
    gap_ref,
    gain_ref,
    decay_ref,
    local_ref,
    out_grad_ref,
    mix_ref,
    ends_ref,
    gain_grad_ref,
):
    rows, width = local_ref.shape
    groups = ends_ref.shape[0] // 2
    slots = rows // (2 * groups)
    gain_grad_ref[...] = jnp.zeros_like(gain_grad_ref)

    def gates(at):
        scale = scale_ref[at, :]
        out_logit = logits_ref[at, pl.ds(2 * width, width)]
        closed = 1.0 - jax.nn.sigmoid(logits_ref[at, pl.ds(width, width)])
        decay_ref[at, :] = 1.0 - gap_ref[...] * closed * valid_ref[at, :]
        squashed = jax.nn.sigmoid(out_logit)
        swish = out_logit * squashed
        slope = squashed * (1.0 + out_logit * (1.0 - squashed))
        normed = hidden_ref[at, :] * scale
        grad_mix = grad_mix_ref[at, :]
        through = grad_mix * normed
        gain_grad_ref[...] += jnp.sum(through * swish, axis=0, keepdims=True)
        out_grad_ref[at, :] = (through * gain_ref[...] * slope).astype(bf16)
        mix_ref[at, :] = (normed * gain_ref[...] * swish).astype(bf16)
        local_ref[at, :] = scale * (grad_mix * gain_ref[...] * swish - normed * mean_ref[at, :])

    by_chunks(rows, gates)
    tiles = 2 * slots // TILE

    def step(k, carried):
        first = tile_row(tiles - 1 - k, TILE, core_ref[0], slots, groups)
        after_tile = []
        for b, (carry_decay, carry, later) in enumerate(carried):
            at = tile_at(first, b, TILE, slots)
            forget = decay_ref[at, :]
            place = lax.broadcasted_iota(jnp.int32, forget.shape, 0)
            decay = jnp.where(place < TILE - 1, pltpu.roll(forget, TILE - 1, 0), later)
            decay, local = tile_scan(decay, local_ref[at, :], True)
            adjoint = local + decay * carry
            decay = decay * carry_decay
            decay_ref[at, :] = decay
            local_ref[at, :] = adjoint
            after_tile.append((decay[:1, :], adjoint[:1, :], forget[:1, :]))
        return tuple(after_tile)

    one = jnp.ones((1, width), f32)
    ends = lax.fori_loop(0, tiles, step, ((one, jnp.zeros((1, width), f32), one),) * groups)
    ends_ref[...] = jnp.concatenate(
        [end[0] * end[2] for end in ends] + [end[1] * end[2] for end in ends], axis=0
    )


def recur_finish_kernel(
    logits_ref,
    before_ref,
    valid_ref,
    decay_ref,
    local_ref,
    carry_ref,
    out_grad_ref,
    gap_ref,
    grad_ref,
):
    rows, width = local_ref.shape
    groups = carry_ref.shape[0]
    slots = rows // (2 * groups)

    def step(i, nothing):
        for block in range(2 * groups):
            at = pl.ds(pl.multiple_of(block * slots + i * WIDE, WIDE), WIDE)
            carry = carry_ref[block % groups : block % groups + 1, :]
            adjoint = local_ref[at, :] + decay_ref[at, :] * carry
            in_logit = logits_ref[at, pl.ds(0, width)]
            squashed = jax.nn.sigmoid(logits_ref[at, pl.ds(width, width)])
            in_squashed = jax.nn.sigmoid(in_logit)
            in_slope = in_squashed * (1.0 + in_logit * (1.0 - in_squashed))
            weighted = gap_ref[...] * valid_ref[at, :] * (1.0 - squashed) * adjoint
            into = (weighted * in_slope).astype(bf16)
            forget = weighted * squashed * (before_ref[at, :] - in_logit * in_squashed)
            grad_ref[at, :] = jnp.concatenate(
                [into, forget.astype(bf16), out_grad_ref[at, :]], axis=1
            )
        return nothing

    lax.fori_loop(0, slots // WIDE, step, 0)


def finish_input_kernel(groups, chips, tokens_ref, gains_ref, residual_ref, *refs):
    part_refs, grad_ref, gain_grad_ref = refs[:-2], refs[-2], refs[-1]
    total = part_refs[0][...].astype(f32)
    for part_ref in part_refs[1:]:
        total = total + part_ref[...].astype(f32)
    piece = total.shape[1] // (groups * chips)
    grad = jnp.concatenate(
        [
            total[:, (z * groups + g) * piece : (z * groups + g + 1) * piece]
            for g in range(groups)
            for z in range(chips)
        ],
        axis=1,
    )
    inputs = tokens_ref[...].astype(f32)
    scale = rms_scale(inputs)
    normed = inputs * scale
    gain_grad_ref[...] = jnp.sum(grad * normed, axis=0, keepdims=True)
    grad_ref[...] = (
        residual_ref[...] + rms_back(grad * gains_ref[0:1, :], normed, scale)
    ).astype(bf16)


def call_kernel(kernel, name, shapes, scalar, *args):
    specs = [pl.BlockSpec(memory_space=pltpu.VMEM)] * len(args)
    if scalar is not None:
        specs, args = [pl.BlockSpec(memory_space=pltpu.SMEM)] + specs, (scalar,) + args
    return pl.pallas_call(
        kernel,
        out_shape=[jax.ShapeDtypeStruct(shape, kind) for shape, kind in shapes],
        in_specs=specs,
        compiler_params=pltpu.CompilerParams(vmem_limit_bytes=VMEM_BYTES),
        name=name,
    )(*args)


SEQUENCE = ("z", "core")
PLANE = ("dp", "core")


def gather_tokens(part):
    return lax.all_gather(part, SEQUENCE, axis=0, tiled=True)


def scatter_tokens(whole):
    return lax.psum_scatter(whole, SEQUENCE, scatter_dimension=0, tiled=True).astype(f32)


def gather_chips(part):
    return lax.all_gather(part, "z", axis=0, tiled=True)


def scatter_chips(whole):
    return lax.psum_scatter(whole, "z", scatter_dimension=0, tiled=True)


def swap(blocks, axes):
    return lax.all_to_all(blocks, axes, split_axis=0, concat_axis=0, tiled=True)


def gather_plane(part, *earlier):
    near = jnp.concatenate(gather_groups(part), axis=0)
    if earlier:
        near = after(near, *earlier)
    return jnp.concatenate([near, flip(near, "core", 1)], axis=0), near


def scatter_plane(whole, *earlier):
    half, groups = whole.shape[0] // 2, lax.axis_size("dp")
    near = add_low(whole[:half], flip(whole[half:], "core", 1))
    slots = half // groups
    return scatter_groups(
        [near[b * slots : (b + 1) * slots] for b in range(groups)], *earlier
    )


def chain_chips(ends, reverse):
    chips, here = lax.axis_size("z"), lax.axis_index("z")
    count = ends.shape[0] // 2
    carry = jnp.zeros_like(ends[:count])
    for far in range(chips - 1, 0, -1):
        step = -far if reverse else far
        there = lax.ppermute(ends, "z", [(i, (i + step) % chips) for i in range(chips)])
        reached = here + far < chips if reverse else here >= far
        carry = jnp.where(reached, there[count:] + there[:count] * carry, carry)
    return carry


def flip(part, axis, bit):
    count = lax.axis_size(axis)
    return lax.ppermute(part, axis, [(i, i ^ bit) for i in range(count)])


def bits_of(axis):
    return [1 << k for k in range(lax.axis_size(axis).bit_length() - 1)]


def half_rows(rows):
    return -(-rows // 32) * 16


def gather_groups(part, *earlier):
    if lax.axis_size("dp") == 4:
        half = half_rows(part.shape[0])
        one, two = flip(part, "dp", 1), flip(part, "dp", 2)
        if earlier:
            one, two = after(one, *earlier), after(two, *earlier)
        three = jnp.concatenate(
            [flip(one[:half], "dp", 2), flip(two[half:], "dp", 1)], axis=0
        )
        return [part, one, two, three]
    blocks = [part]
    for bit in bits_of("dp"):
        blocks = blocks + [flip(block, "dp", bit) for block in blocks]
    return blocks


def scatter_groups(blocks, *earlier):
    if len(blocks) == 4:
        half = half_rows(blocks[0].shape[0])
        upper = flip(blocks[3][:half], "dp", 1)
        lower = flip(blocks[3][half:], "dp", 2)
        two = jnp.concatenate([add_low(blocks[2][:half], upper), blocks[2][half:]], axis=0)
        one = jnp.concatenate([blocks[1][:half], add_low(blocks[1][half:], lower)], axis=0)
        if earlier:
            one, two = after(one, *earlier), after(two, *earlier)
        return [blocks[0], flip(one, "dp", 1), flip(two, "dp", 2)]
    for bit in reversed(bits_of("dp")):
        blocks = [
            add_low(block, flip(other, "dp", bit))
            for block, other in zip(blocks[:bit], blocks[bit:])
        ]
    return blocks


def add_parts(parts):
    total = parts[0].astype(f32)
    for part in parts[1:]:
        total = total + part.astype(f32)
    return total


def add_low(left, right):
    return (left.astype(f32) + right.astype(f32)).astype(bf16)


def sum_over(part, axes):
    for axis in axes:
        for bit in bits_of(axis):
            part = part + flip(part, axis, bit)
    return part


def place_groups(blocks):
    group, rows = lax.axis_index("dp"), blocks[0].shape[0]
    whole = jnp.zeros((len(blocks) * rows,) + blocks[0].shape[1:], blocks[0].dtype)
    for b, block in enumerate(blocks):
        whole = lax.dynamic_update_slice_in_dim(whole, block, (group ^ b) * rows, 0)
    return whole


def take_groups(whole, axis):
    count, group = lax.axis_size("dp"), lax.axis_index("dp")
    size = whole.shape[axis] // count
    return [
        lax.dynamic_slice_in_dim(whole, (group ^ b) * size, size, axis) for b in range(count)
    ]


def sequence_pieces():
    groups, peers = lax.axis_size("dp"), lax.axis_size("z") * 2
    return [[g * peers + j for g in range(groups)] for j in range(peers)]


def plane_pieces():
    groups, chips = lax.axis_size("dp"), lax.axis_size("z")
    return [
        [(g * chips + z) * 2 + core for z in range(chips)]
        for g in range(groups)
        for core in range(2)
    ]


def split_kernel(kinds, piece, table, weight_ref, split_ref, *rest_refs):
    rows, every, depth = weight_ref.shape
    whole = [weight_ref[:, k, :] for k in range(every)]
    for j, pieces in enumerate(table):
        own = [
            whole[k][:, p * piece : (p + 1) * piece] for k in range(kinds) for p in pieces
        ]
        split_ref[j * rows : (j + 1) * rows, :] = jnp.concatenate(own, axis=1).astype(bf16)
    for k, rest_ref in zip(range(kinds, every), rest_refs):
        part = depth // len(table)
        for j in range(len(table)):
            rest_ref[j * rows : (j + 1) * rows, :] = whole[k][
                :, j * part : (j + 1) * part
            ].astype(bf16)


def split_columns(weight, kinds, piece, table):
    rows, every, depth = weight.shape
    shapes = [jax.ShapeDtypeStruct((len(table) * rows, kinds * len(table[0]) * piece), bf16)]
    shapes += [
        jax.ShapeDtypeStruct((len(table) * rows, depth // len(table)), bf16)
    ] * (every - kinds)
    return pl.pallas_call(
        functools.partial(split_kernel, kinds, piece, table),
        out_shape=shapes,
        compiler_params=pltpu.CompilerParams(vmem_limit_bytes=VMEM_BYTES),
        name="split_columns",
    )(weight)


def join_kernel(kinds, piece, table, own_ref, *refs):
    rest_refs, out_ref = refs[:-1], refs[-1]
    rows, every, depth = out_ref.shape
    place = {p: (j, q) for j, pieces in enumerate(table) for q, p in enumerate(pieces)}
    count = len(table[0])
    own = [own_ref[j * rows : (j + 1) * rows, :].astype(f32) for j in range(len(table))]
    for k in range(kinds):
        pieces = []
        for p in range(len(place)):
            j, q = place[p]
            pieces.append(own[j][:, (k * count + q) * piece : (k * count + q + 1) * piece])
        out_ref[:, k, :] = jnp.concatenate(pieces, axis=1)
    for k, rest_ref in zip(range(kinds, every), rest_refs):
        out_ref[:, k, :] = rest_ref[...]


def join_columns(own, kinds, piece, table, *rest):
    shape = (own.shape[0] // len(table), kinds + len(rest), len(table) * len(table[0]) * piece)
    return pl.pallas_call(
        functools.partial(join_kernel, kinds, piece, table),
        out_shape=jax.ShapeDtypeStruct(shape, f32),
        compiler_params=pltpu.CompilerParams(vmem_limit_bytes=VMEM_BYTES),
        name="join_columns",
    )(own, *rest)


def after_kernel(*refs):
    pass


def after(value, *earlier):
    return pl.pallas_call(
        after_kernel,
        out_shape=jax.ShapeDtypeStruct(value.shape, value.dtype),
        in_specs=[pl.BlockSpec(memory_space=pl.ANY)] * (1 + len(earlier)),
        out_specs=pl.BlockSpec(memory_space=pl.ANY),
        input_output_aliases={0: 0},
        name="after",
    )(value, *earlier)


def dot(left, right, dims):
    return lax.dot_general(left, right, (dims, ((), ())), preferred_element_type=f32)


def body(
    tokens,
    out_cotangent,
    counts,
    forget_gap,
    mixer_weight,
    expand_weight,
    shrink_weight,
    norm_gains,
    mixer_first,
    mixer_second,
    expand_first,
    expand_second,
    shrink_first,
    shrink_second,
    gains_first,
    gains_second,
):
    nd, chips = lax.axis_size("dp"), lax.axis_size("z")
    group, core = lax.axis_index("dp"), lax.axis_index("core")
    slots, depth = tokens.shape
    rows = mixer_weight.shape[0]
    hid_rows = shrink_weight.shape[0]
    width = chips * rows
    hid = nd * hid_rows
    plane_rows = 2 * nd * slots
    core_low = core.astype(jnp.int32).reshape(1)

    def own_columns(vector):
        pieces = vector.reshape(nd, chips, 2, rows)
        return lax.dynamic_slice(pieces, (group, 0, core, 0), (1, chips, 1, rows)).reshape(1, width)

    def turn(whole, first, second):
        pieces = whole.reshape(slots, first, second, 2 * rows)
        return pieces.transpose(0, 2, 1, 3).reshape(slots, depth)

    lead_blocks, trail_low = split_columns(mixer_weight, 3, rows, plane_pieces())
    (expand_blocks,) = split_columns(expand_weight, 2, hid_rows, sequence_pieces())

    valid_here = (lax.iota(jnp.int32, slots) < counts[0, 0]).astype(f32)[:, None]
    inputs = tokens.astype(f32)
    scale_one = rms_scale(inputs)
    normed_one = inputs * scale_one
    input_low = turn((normed_one * norm_gains[0]).astype(bf16), nd, chips)
    cotangent_low = (out_cotangent.astype(f32) * valid_here).astype(bf16)

    lead_own = swap(lead_blocks, PLANE)
    input_low = jnp.concatenate([input_low, pad_columns(valid_here.astype(bf16))], axis=1)
    input_all, _ = gather_plane(after(input_low, lead_own))
    valid = input_all[:, depth : depth + 1].astype(f32)
    input_all = input_all[:, :depth]
    shrink = place_groups(gather_groups(after(shrink_weight.astype(bf16), valid)))
    mixer_own = jnp.concatenate([lead_own, trail_low], axis=1)
    cotangent_all = gather_tokens(cotangent_low)
    mixer_near = gather_chips(after(mixer_own, cotangent_all))
    mixer_near = after(mixer_near, expand_blocks, valid, shrink)
    lead = mixer_near[:, : 3 * width]
    trail = mixer_near[:, 3 * width :].reshape(chips, 2 * nd, rows, width)
    trail = trail.transpose(0, 2, 1, 3).reshape(width, depth)

    gap = own_columns(forget_gap)
    gain = own_columns(norm_gains[1])
    logits = dot(input_all, lead, ((1,), (0,)))
    square, low_square = ((plane_rows, width), f32), ((plane_rows, width), bf16)
    ends_shape = ((2 * nd, width), f32)
    decay, local, ends = call_kernel(
        recur_forward_kernel,
        "recur_forward",
        [square, square, ends_shape],
        core_low,
        logits,
        valid,
        gap,
    )
    carry = chain_chips(ends, False)
    expand_own = swap(after(expand_blocks, carry), SEQUENCE)
    hidden, before, mix, squares = call_kernel(
        recur_mix_kernel,
        "recur_mix",
        [square, square, low_square, ((plane_rows, 1), f32)],
        core_low,
        logits,
        decay,
        local,
        carry,
        gain,
    )
    mixed_part = dot(mix, trail, ((1,), (0,))).astype(bf16)
    mixed_part = jnp.concatenate([mixed_part, pad_columns(split_low(squares))], axis=1)
    mixed_sum = add_parts(scatter_plane(mixed_part, expand_own))
    expand = place_groups(gather_groups(expand_own))
    scale_two = lax.rsqrt(
        (mixed_sum[:, depth : depth + 1] + mixed_sum[:, depth + 1 : depth + 2]) / depth + norm_eps
    )
    mixed = mixed_sum[:, :depth] * scale_two
    residual = inputs + mixed
    scale_three = rms_scale(residual)
    normed_three = residual * scale_three
    feed_low = (normed_three * norm_gains[2]).astype(bf16)
    feed_all = gather_tokens(feed_low)
    expanded = dot(feed_all, expand, ((1,), (0,)))
    gate, up = expanded[:, :hid], expanded[:, hid:]
    gate_silu = jax.nn.silu(gate)
    product_low = (gate_silu * up).astype(bf16)
    grad_product = dot(cotangent_all, shrink, ((1,), (1,)))
    grad_expanded = jnp.concatenate(
        [grad_product * up * silu_slope(gate), grad_product * gate_silu], axis=1
    ).astype(bf16)
    feed_part = dot(grad_expanded, expand, ((1,), (1,))).astype(bf16)
    grad_feed = scatter_tokens(feed_part)
    gain_three = jnp.sum(grad_feed * normed_three, 0)
    grad_residual = cotangent_low.astype(f32) + rms_back(
        grad_feed * norm_gains[2], normed_three, scale_three
    )
    residual_low = grad_residual.astype(bf16)
    mean_two = jnp.mean(residual_low.astype(f32) * mixed, axis=-1, keepdims=True)
    extras = pad_columns(jnp.concatenate([split_low(scale_two), split_low(mean_two)], axis=1))

    def owner_parts(left, right):
        return [
            dot(block, right, ((0,), (0,))).astype(bf16) for block in take_groups(left, 1)
        ]

    expand_sum = add_parts(scatter_groups(owner_parts(feed_all, grad_expanded))).astype(bf16)
    expand_columns = swap(expand_sum, SEQUENCE)
    back_all, back_near = gather_plane(
        after(jnp.concatenate([residual_low, extras], axis=1), expand_sum), expand_columns
    )
    out_part = dot(product_low, shrink, ((1,), (0,))).astype(bf16)
    out_sum = scatter_tokens(after(out_part, back_near))
    block_output = ((residual + out_sum) * valid_here).astype(bf16)
    residual_back = back_all[:, :depth]
    extras = back_all[:, depth : depth + 4].astype(f32)
    scale_all = extras[:, 0:1] + extras[:, 1:2]
    mean_all = extras[:, 2:3] + extras[:, 3:4]

    grad_mix = dot(residual_back, trail, ((1,), (1,)))
    decay, local, out_grad, mix_low, ends, gain_two = call_kernel(
        recur_reverse_kernel,
        "recur_reverse",
        [square, square, low_square, low_square, ends_shape, ((1, width), f32)],
        core_low,
        logits,
        hidden,
        grad_mix,
        valid,
        scale_all,
        mean_all,
        gap,
        gain,
    )
    carry = chain_chips(ends, True)
    (grad_projected,) = call_kernel(
        recur_finish_kernel,
        "recur_finish",
        [((plane_rows, 3 * width), bf16)],
        None,
        logits,
        before,
        valid,
        decay,
        local,
        carry,
        out_grad,
        gap,
    )
    trail_part = dot(mix_low, residual_back, ((0,), (0,))).astype(bf16)
    lead_part = dot(input_all, grad_projected, ((0,), (0,))).astype(bf16)
    lead_part = after(lead_part, out_sum)
    lead_sum = scatter_chips(lead_part)
    trail_grad = scatter_chips(after(trail_part, lead_sum))
    input_part = dot(after(grad_projected, lead_part), lead, ((1,), (1,))).astype(bf16)
    input_parts = scatter_plane(input_part)
    token_grad, gain_one = call_kernel(
        functools.partial(finish_input_kernel, nd, chips),
        "finish_input",
        [((slots, depth), bf16), ((1, depth), f32)],
        None,
        tokens,
        norm_gains,
        grad_residual,
        *input_parts,
    )
    gain_one = gain_one[0]
    shrink_part = dot(product_low, after(cotangent_all, input_part), ((0,), (0,))).astype(bf16)
    shrink_grad = add_parts(scatter_groups(take_groups(shrink_part, 0)))

    expand_grad = join_columns(
        after(expand_columns, input_part), 2, hid_rows, sequence_pieces()
    )
    lead_columns = swap(lead_sum, PLANE)

    gain_two_full = lax.dynamic_update_slice(
        jnp.zeros((nd, chips, 2, rows), f32),
        gain_two.reshape(1, chips, 1, rows),
        (group, 0, core, 0),
    ).reshape(depth)
    mixer_grad = join_columns(lead_columns, 3, rows, plane_pieces(), trail_grad.astype(f32))
    expand_first_new, expand_second_new, expand_update = adam_direction(
        expand_weight, expand_grad, expand_first, expand_second
    )
    shrink_first_new, shrink_second_new, shrink_update = adam_direction(
        shrink_weight, shrink_grad, shrink_first, shrink_second
    )
    mixer_first_new, mixer_second_new, mixer_update = adam_direction(
        mixer_weight, mixer_grad, mixer_first, mixer_second
    )
    squares_here = jnp.concatenate(
        [
            squares_of(mixer_weight),
            squares_of(expand_weight),
            squares_of(shrink_weight[:, None]),
            squares_of(mixer_update),
            squares_of(expand_update),
            squares_of(shrink_update[:, None]),
        ]
    )
    summed = sum_over(
        after(
            jnp.stack([gain_one, gain_two_full, gain_three, jnp.pad(squares_here, (0, depth - 14))]),
            block_output,
        ),
        ("dp", "z", "core"),
    )
    gains_grad = summed[:3]
    weight_sq, update_sq = summed[3, :7], summed[3, 7:14]
    gains_first_new, gains_second_new, gains_update = adam_direction(
        norm_gains, gains_grad, gains_first, gains_second
    )
    mixer_weight_new = apply_trust(
        mixer_weight, mixer_update, weight_sq[0:4], update_sq[0:4], (1, 4, 1)
    )
    expand_weight_new = apply_trust(
        expand_weight, expand_update, weight_sq[4:6], update_sq[4:6], (1, 2, 1)
    )
    shrink_weight_new = apply_trust(
        shrink_weight, shrink_update, weight_sq[6], update_sq[6], (1, 1)
    )
    gain_weight_sq = jnp.sum(norm_gains * norm_gains, axis=1)
    gain_update_sq = jnp.sum(gains_update * gains_update, axis=1)
    gains_new = apply_trust(norm_gains, gains_update, gain_weight_sq, gain_update_sq, (3, 1))
    weight_norms = jnp.sqrt(jnp.concatenate([weight_sq, gain_weight_sq]))
    update_norms = jnp.sqrt(jnp.concatenate([update_sq, gain_update_sq]))
    trust_norms = jnp.stack([weight_norms, update_norms])
    return (
        block_output,
        token_grad,
        mixer_grad,
        mixer_first_new,
        mixer_second_new,
        mixer_weight_new,
        expand_grad,
        expand_first_new,
        expand_second_new,
        expand_weight_new,
        shrink_grad,
        shrink_first_new,
        shrink_second_new,
        shrink_weight_new,
        gains_grad,
        gains_first_new,
        gains_second_new,
        gains_new,
        trust_norms,
    )


def solution(mesh):
    groups, peers = mesh.devices.shape
    devices = mesh.devices.reshape(groups, peers // 2, 2)
    return jax.shard_map(
        body,
        mesh=jax.sharding.Mesh(devices, ("dp", "z", "core")),
        in_specs=(
            P(("dp", "z", "core"), None),
            P(("dp", "z", "core"), None),
            P("dp", ("z", "core")),
            P(),
            P(("dp", "z", "core"), None, None),
            P(("dp", "z", "core"), None, None),
            P(("dp", "z", "core"), None),
            P(),
            P(("dp", "z", "core"), None, None),
            P(("dp", "z", "core"), None, None),
            P(("dp", "z", "core"), None, None),
            P(("dp", "z", "core"), None, None),
            P(("dp", "z", "core"), None),
            P(("dp", "z", "core"), None),
            P(),
            P(),
        ),
        out_specs=(
            P(("dp", "z", "core"), None),
            P(("dp", "z", "core"), None),
            P(("dp", "z", "core"), None, None),
            P(("dp", "z", "core"), None, None),
            P(("dp", "z", "core"), None, None),
            P(("dp", "z", "core"), None, None),
            P(("dp", "z", "core"), None, None),
            P(("dp", "z", "core"), None, None),
            P(("dp", "z", "core"), None, None),
            P(("dp", "z", "core"), None, None),
            P(("dp", "z", "core"), None),
            P(("dp", "z", "core"), None),
            P(("dp", "z", "core"), None),
            P(("dp", "z", "core"), None),
            P(),
            P(),
            P(),
            P(),
            P(),
        ),
        check_vma=False,
    )
```

time: 2920 us -> 625 us (0.21)
  waiting for transfers between devices: 2160 us -> 275 us
  local copies, waits for them, and re-layouts: 284 us -> 61.4 us
  matrix products: 192 us -> 80.6 us
  blocking collectives: 80 us -> 0 us
  other arithmetic: 166 us -> 87.9 us
  starting transfers between devices: 0.42 us -> 65.5 us
    reduce_scatter x3 -> x4, waiting for transfers between devices: 1720 us -> 15.7 us  [the longest x2 9.07 us: scatter_chips(): return lax.psum_scatter(whole, 'z', scatter_dimension=0, tiled=True)]
    all_gather x3, waiting for transfers between devices: 440 us -> 56.2 us  [the longest x1 31.3 us: gather_chips(): return lax.all_gather(part, 'z', axis=0, tiled=True)]
    ppermute x0 -> x47, waiting for transfers between devices: none -> 171 us  [the longest x41 168 us: flip(): return lax.ppermute(part, axis, [(i, i ^ bit) for i in range(count)])]
    slice x95 -> x19, local copies, waits for them, and re-layouts: 170 us -> 11.2 us  [the longest x4 2.23 us: gather_groups(): one[:half]]
    dot_general x12 -> x15, matrix products: 192 us -> 80.6 us  [dot(): lax.dot_general(left, right, (dims, ((), ())), preferred_element_type=f32)]
    pad x48 -> x1, local copies, waits for them, and re-layouts: 49.8 us -> 0.01 us  [body(): jnp.pad(squares_here, (0, depth - 14))]
    ppermute x0 -> x47, starting transfers between devices: none -> 47 us  [the longest x41 41.1 us: flip(): return lax.ppermute(part, axis, [(i, i ^ bit) for i in range(count)])]
    all_gather x3 -> x0, blocking collectives: 42.9 us -> none  [prefix(): everything = jax.tree.map(lambda part: lax.all_gather(part, axis), array)]
  transfers between devices with their start and end apart: 6 -> 58, of which waited for: 6 -> 36; matrix products, arithmetic and copies ran while one was open for 19% -> 22% of each run, Pallas kernels for 0% -> 3%
where the time goes in v1:
time: 625 us; the launch traced here: 614 us
  waiting for transfers between devices  275 us (44%)
  other arithmetic  87.9 us (14%)
  matrix products  80.6 us (13%)
  starting transfers between devices  65.5 us (10%)
  local copies, waits for them, and re-layouts  61.4 us (10%)
  Pallas kernels  26.4 us (4%)
  between operations  17.8 us (3%)
    ppermute x41, waiting for transfers between devices, flip(): return lax.ppermute(part, axis, [(i, i ^ bit) for i in range(count)])  168 us
    dot_general x15, matrix products, dot(): lax.dot_general(left, right, (dims, ((), ())), preferred_element_type=f32)  80.6 us
    ppermute x41, starting transfers between devices, flip(): return lax.ppermute(part, axis, [(i, i ^ bit) for i in range(count)])  41.1 us
    all_to_all x4, waiting for transfers between devices, swap(): return lax.all_to_all(blocks, axes, split_axis=0, concat_axis=0, tiled=True)  31.9 us
    all_gather x1, waiting for transfers between devices, gather_chips(): return lax.all_gather(part, 'z', axis=0, tiled=True)  31.3 us
    unnamed x145, local copies, waits for them, and re-layouts  30.9 us
    reduce_sum x3, other arithmetic, squares_of(): return jnp.sum(matrices * matrices, axis=(0, 2))  27 us
    all_gather x2, waiting for transfers between devices, gather_tokens(): return lax.all_gather(part, SEQUENCE, axis=0, tiled=True)  24.9 us
  transfers between devices with their start and end apart: 58, of which 36 were waited for; matrix products, arithmetic and copies ran while one was open for 22% of the time, Pallas kernels for 3%

profile of v1, /device:TPU:0, one launch (start us, length us, event | category | flops | bytes accessed | tf_op | source)
XLA Modules:
  0.0 614.2 jit_solution(5828655720267290289)
XLA Ops:
  13.1 5.2 all-to-all-start
  20.6 10.3 %all-to-all-done = bf16[8,64,768]{2,1,0:T(8,128)(2,1)S(1)} async-done(((bf16[8,64,768]{2,1,0:T(8,128)(2,1)}), bf16[8,64,768]{2,1,0:T(8,128)(2,1)S(1)}, u32[]{:S(2)}, u32[]{:S(2)}) %all-to-all-start) | async-done | bytes 786464 | tf_op jit(solution)/shard_map/all_to_all | solution.py:331
  35.2 24.9 %all-gather.4.cloned.1.call-done.refs_1_.refs_0_ = bf16[1024,2048]{1,0:T(8,128)(2,1)} async-done(((bf16[128,2048]{1,0:T(8,128)(2,1)}), bf16[1024,2048]{1,0:T(8,128)(2,1)}) %all-gather.4.cloned.1.call-update) | async-done | bytes 4194320 | tf_op jit(solution)/shard_map/all_gather | solution.py:315
  63.6 5.5 collective-permute-done.2
  84.1 12.5 %collective-permute-done.6 = bf16[176,2048]{1,0:T(8,128)(2,1)} collective-permute-done((bf16[176,2048]{1,0:T(8,128)(2,1)}, bf16[176,2048]{1,0:T(8,128)(2,1)}, u32[]{:S(2)}, u32[]{:S(2)}) %collective-permute-start.6) | collective-permute-done | bytes 720928 | tf_op jit(solution)/shard_map/ppermute | solution.py:364
  110.4 31.3 %all-gather.6.cloned.1.call-done.refs_0_ = bf16[2048,1024]{1,0:T(8,128)(2,1)} async-done(((bf16[512,1024]{1,0:T(8,128)(2,1)}), bf16[2048,1024]{1,0:T(8,128)(2,1)}) %all-gather.6.cloned.1.call-update) | async-done | bytes 4194320 | tf_op jit(solution)/shard_map/all_gather | solution.py:323
  141.7 6.2 %fusion.3.logits_ref = f32[1024,768]{1,0:T(8,128)S(1)} fusion(bf16[1024,2176]{1,0:T(8,128)(2,1)} %copy-done.58, bf16[2048,1024]{1,0:T(8,128)(2,1)} %after.19), kind=kOutput, calls=%fused_computation.14 | convolution fusion | flops 3221225472 | bytes 10485760 | tf_op jit(solution)/shard_map/dot_general | solution.py:529
  179.5 5.7 collective-permute-done.13
  188.3 19.3 %all-to-all-done.1 = bf16[8,64,1408]{2,1,0:T(8,128)(2,1)S(1)} async-done(((bf16[8,64,1408]{2,1,0:T(8,128)(2,1)}), bf16[8,64,1408]{2,1,0:T(8,128)(2,1)S(1)}, u32[]{:S(2)}, u32[]{:S(2)}) %all-to-all-start.1) | async-done | bytes 1441824 | tf_op jit(solution)/shard_map/all_to_all | solution.py:331
  211.7 11.4 %collective-permute-done.16 = bf16[128,2176]{1,0:T(8,128)(2,1)S(1)} collective-permute-done((bf16[128,2176]{1,0:T(8,128)(2,1)}, bf16[128,2176]{1,0:T(8,128)(2,1)S(1)}, u32[]{:S(2)}, u32[]{:S(2)}) %collective-permute-start.16) | collective-permute-done | bytes 557088 | tf_op jit(solution)/shard_map/ppermute | solution.py:364
  232.2 30.0 %collective-permute-done.18 = bf16[512,1408]{1,0:T(8,128)(2,1)} collective-permute-done((bf16[512,1408]{1,0:T(8,128)(2,1)S(1)}, bf16[512,1408]{1,0:T(8,128)(2,1)}, u32[]{:S(2)}, u32[]{:S(2)}) %collective-permute-start.18) | collective-permute-done | bytes 1441824 | tf_op jit(solution)/shard_map/ppermute | solution.py:364
  282.6 10.6 %fusion.86 = f32[1024,1408]{1,0:T(8,128)S(1)} fusion(bf16[1024,2048]{1,0:T(8,128)(2,1)} %all-gather.8.cloned.1.call-done, bf16[2048,1408]{1,0:T(8,128)(2,1)} %maximum_dynamic-update-slice_fusion), kind=kOutput, calls=%fused_computation.224 | convolution fusion | flops 5905580032 | bytes 15728640 | tf_op jit(solution)/shard_map/dot_general | solution.py:529
  293.2 5.4 multiply_convert_fusion.1
  300.3 11.3 %convolution_convert_fusion = bf16[1024,2048]{1,0:T(8,128)(2,1)} fusion(bf16[2048,1408]{1,0:T(8,128)(2,1)} %maximum_dynamic-update-slice_fusion, bf16[1024,704]{1,0:T(8,128)(2,1)S(1)} %get-tuple-element.79, bf16[1024,704]{1,0:T(8,128)(2,1)S(1)} %get-tuple-element.78), kind=kOutput, calls=%fused_computation.8 | convolution fusion | flops 5913444352 | bytes 12845056 | tf_op jit(solution)/shard_map/dot_general | solution.py:529
  321.8 8.6 %collective-permute-done.23 = bf16[256,1408]{1,0:T(8,128)(2,1)S(1)} collective-permute-done((bf16[256,1408]{1,0:T(8,128)(2,1)S(1)}, bf16[256,1408]{1,0:T(8,128)(2,1)S(1)}, u32[]{:S(2)}, u32[]{:S(2)}) %collective-permute-start.23) | collective-permute-done | bytes 720928 | tf_op jit(solution)/shard_map/ppermute | solution.py:364
  331.4 6.9 %collective-permute-done.21 = bf16[256,1408]{1,0:T(8,128)(2,1)S(1)} collective-permute-done((bf16[256,1408]{1,0:T(8,128)(2,1)S(1)}, bf16[256,1408]{1,0:T(8,128)(2,1)S(1)}, u32[]{:S(2)}, u32[]{:S(2)}) %collective-permute-start.21) | collective-permute-done | bytes 720928 | tf_op jit(solution)/shard_map/ppermute | solution.py:364
  341.2 23.3 %collective-permute-done.24 = bf16[512,1408]{1,0:T(8,128)(2,1)S(1)} collective-permute-done((bf16[512,1408]{1,0:T(8,128)(2,1)S(1)}, bf16[512,1408]{1,0:T(8,128)(2,1)S(1)}, u32[]{:S(2)}, u32[]{:S(2)}) %collective-permute-start.24) | collective-permute-done | bytes 1441824 | tf_op jit(solution)/shard_map/ppermute | solution.py:364
  379.5 7.7 %convolution_convert_fusion.1.refs_0_ = bf16[1024,2048]{1,0:T(8,128)(2,1)} fusion(bf16[1024,704]{1,0:T(8,128)(2,1)} %get-tuple-element.80, bf16[704,2048]{1,0:T(8,128)(2,1)} %copy-done.40), kind=kOutput, calls=%fused_computation.9 | convolution fusion | flops 2954887168 | bytes 8519680 | tf_op jit(solution)/shard_map/dot_general | solution.py:529
  388.1 5.3 collective-permute-done.25
  396.9 4.8 collective-permute-done.27
  406.7 4.7 collective-permute-done.29
  418.2 6.1 recur_reverse.1
  439.9 8.1 %fusion.5.refs_0_ = bf16[2048,768]{1,0:T(8,128)(2,1)} fusion(bf16[1024,768]{1,0:T(8,128)(2,1)S(1)} %recur_finish.1.refs_0_, bf16[1024,2176]{1,0:T(8,128)(2,1)} %copy-done.58), kind=kOutput, calls=%fused_computation.16 | convolution fusion | flops 3222798336 | bytes 8912896 | tf_op jit(solution)/shard_map/dot_general | solution.py:529
  448.0 6.6 %reduce-scatter.7.cloned.1.call-done = bf16[128,2048]{1,0:T(8,128)(2,1)} async-done(((bf16[1024,2048]{1,0:T(8,128)(2,1)}), bf16[128,2048]{1,0:T(8,128)(2,1)}) %reduce-scatter.7.cloned.1.call-update) | async-done | bytes 524304 | tf_op jit(solution)/shard_map/reduce_scatter | solution.py:319
  458.1 5.6 convolution_convert_fusion.3.refs_1_
  472.5 5.6 convolution_convert_fusion.4
  482.7 12.9 %multiply_reduce_fusion = (f32[2]{0:T(128)S(1)}, f32[64,2,5632]{2,1,0:T(2,128)}, f32[64,2,5632]{2,1,0:T(2,128)}, f32[64,2,5632]{2,1,0:T(2,128)}, f32[2]{0:T(128)S(1)}) fusion(f32[64,2,5632]{2,1,0:T(2,128)S(1)} %copy-done.2, f32[64,2,5632]{2,1,0:T(2,128)S(1)} %copy-done.38, f32[64,2,5632]{2,1,0:T(2,128)S(1)} %copy-done.53, f32[64,2,5632]{2,1,0:T(2,128)S(1)} %copy-done.54), kind=kLoop, calls=%fused_computation.32 | loop fusion | flops 12255228 | bytes 20185104 | tf_op jit(solution)/shard_map/reduce_sum | solution.py:44
  506.2 9.1 %reduce-scatter.9.cloned.1.call-done.refs_1_ = bf16[512,768]{1,0:T(8,128)(2,1)} async-done(((bf16[2048,768]{1,0:T(8,128)(2,1)}), bf16[512,768]{1,0:T(8,128)(2,1)}) %reduce-scatter.9.cloned.1.call-update) | async-done | bytes 786448 | tf_op jit(solution)/shard_map/reduce_scatter | solution.py:327
  537.8 6.2 %multiply_reduce_fusion.4 = (f32[]{:T(128)}, f32[]{:T(128)}, f32[176,2048]{1,0:T(8,128)}, f32[176,2048]{1,0:T(8,128)}, f32[176,2048]{1,0:T(8,128)}) fusion(f32[176,2048]{1,0:T(8,128)} %param.22, f32[176,2048]{1,0:T(8,128)} %param.28, f32[176,2048]{1,0:T(8,128)} %param.29, bf16[176,2048]{1,0:T(8,128)(2,1)} %collective-permute-done.41, ...), kind=kLoop, calls=%fused_computation.57 | loop fusion | flops 7929854 | bytes 10813452 | tf_op jit(solution)/shard_map/reduce_sum | solution.py:44
  545.1 11.0 %collective-permute-done.37.refs_2_ = bf16[128,2048]{1,0:T(8,128)(2,1)S(1)} collective-permute-done((bf16[128,2048]{1,0:T(8,128)(2,1)S(1)}, bf16[128,2048]{1,0:T(8,128)(2,1)S(1)}, u32[]{:S(2)}, u32[]{:S(2)}) %collective-permute-start.37) | collective-permute-done | bytes 524320 | tf_op jit(solution)/shard_map/ppermute | solution.py:364
  563.2 7.9 %multiply_reduce_fusion.2 = (f32[4]{0:T(128)S(1)}, f32[64,4,2048]{2,1,0:T(4,128)}, f32[64,4,2048]{2,1,0:T(4,128)}, f32[64,4,2048]{2,1,0:T(4,128)}, f32[4]{0:T(128)S(1)}) fusion(f32[64,4,2048]{2,1,0:T(4,128)S(1)} %copy-done.9, f32[64,4,2048]{2,1,0:T(4,128)} %join_columns.2, f32[64,4,2048]{2,1,0:T(4,128)} %param.25, f32[64,4,2048]{2,1,0:T(4,128)} %param.24), kind=kLoop, calls=%fused_computation.45 | loop fusion | flops 8912888 | bytes 14680096 | tf_op jit(solution)/shard_map/reduce_sum | solution.py:44
  594.7 5.0 multiply_subtract_fusion.1
  (400 shorter events, 261.7 us)
Async XLA Ops:
  7.2 52.9 %all-gather.4.cloned.1.call-start = ((), (), s32[]{:S(2)}) async-start(), calls=%async_computation.8 | async-start | bytes 4718592 | tf_op jit(solution)/shard_map/all_gather | solution.py:315
  13.1 17.8 %all-to-all-start = ((bf16[8,64,768]{2,1,0:T(8,128)(2,1)}), bf16[8,64,768]{2,1,0:T(8,128)(2,1)S(1)}, u32[]{:S(2)}, u32[]{:S(2)}) async-start(bf16[8,64,768]{2,1,0:T(8,128)(2,1)} %bitcast.4), calls=%async_computation | async-start | bytes 1572864 | tf_op jit(solution)/shard_map/all_to_all | solution.py:331
  18.3 123.4 %all-gather.6.cloned.1.call-start = ((), (), s32[]{:S(2)}) async-start(), calls=%async_computation.9 | async-start | bytes 5242880 | tf_op jit(solution)/shard_map/all_gather | solution.py:323
  31.8 28.4 %collective-permute-start = (bf16[128,2176]{1,0:T(8,128)(2,1)}, bf16[128,2176]{1,0:T(8,128)(2,1)S(1)}, u32[]{:S(2)}, u32[]{:S(2)}) collective-permute-start(bf16[128,2176]{1,0:T(8,128)(2,1)} %after.16), channel_id=1, source_target_pairs={{0,8},{8,0},{16,24},{24,16},{1,9},{9,1},{17,25},{25,17},{2,10},{10... | collective-permute-start | bytes 1671176 | tf_op jit(solution)/shard_map/ppermute | solution.py:364
  32.3 29.5 %collective-permute-start.1 = (bf16[128,2176]{1,0:T(8,128)(2,1)}, bf16[128,2176]{1,0:T(8,128)(2,1)S(1)}, u32[]{:S(2)}, u32[]{:S(2)}) collective-permute-start(bf16[128,2176]{1,0:T(8,128)(2,1)} %after.16), channel_id=1, source_target_pairs={{0,16},{8,24},{16,0},{24,8},{1,17},{9,25},{17,1},{25,9},{2,18},{10... | collective-permute-start | bytes 1671176 | tf_op jit(solution)/shard_map/ppermute | solution.py:364
  78.2 18.5 %collective-permute-start.6 = (bf16[176,2048]{1,0:T(8,128)(2,1)}, bf16[176,2048]{1,0:T(8,128)(2,1)}, u32[]{:S(2)}, u32[]{:S(2)}) collective-permute-start(bf16[176,2048]{1,0:T(8,128)(2,1)} %after.18), channel_id=1, source_target_pairs={{0,16},{8,24},{16,0},{24,8},{1,17},{9,25},{17,1},{25,9},{2,18},{10... | collective-permute-start | bytes 2162696 | tf_op jit(solution)/shard_map/ppermute | solution.py:364
  78.7 20.5 %collective-permute-start.5 = (bf16[176,2048]{1,0:T(8,128)(2,1)}, bf16[176,2048]{1,0:T(8,128)(2,1)}, u32[]{:S(2)}, u32[]{:S(2)}) collective-permute-start(bf16[176,2048]{1,0:T(8,128)(2,1)} %after.18), channel_id=1, source_target_pairs={{0,8},{8,0},{16,24},{24,16},{1,9},{9,1},{17,25},{25,17},{2,10},{10... | collective-permute-start | bytes 2162696 | tf_op jit(solution)/shard_map/ppermute | solution.py:364
  168.9 38.7 %all-to-all-start.1 = ((bf16[8,64,1408]{2,1,0:T(8,128)(2,1)}), bf16[8,64,1408]{2,1,0:T(8,128)(2,1)S(1)}, u32[]{:S(2)}, u32[]{:S(2)}) async-start(bf16[8,64,1408]{2,1,0:T(8,128)(2,1)} %bitcast.56), calls=%async_computation.1 | async-start | bytes 2883584 | tf_op jit(solution)/shard_map/all_to_all | solution.py:331
  172.7 109.9 %all-gather.8.cloned.1.call-start = ((), (), s32[]{:S(2)}) async-start(), calls=%async_computation.10 | async-start | bytes 4718592 | tf_op jit(solution)/shard_map/all_gather | solution.py:315
  230.0 140.7 %reduce-scatter.5.cloned.1.call-start = ((), (), s32[]{:S(2)}) async-start(), calls=%async_computation.11 | async-start | bytes 4718592 | tf_op jit(solution)/shard_map/reduce_scatter | solution.py:319
  230.1 32.1 %collective-permute-start.18 = (bf16[512,1408]{1,0:T(8,128)(2,1)S(1)}, bf16[512,1408]{1,0:T(8,128)(2,1)}, u32[]{:S(2)}, u32[]{:S(2)}) collective-permute-start(bf16[512,1408]{1,0:T(8,128)(2,1)S(1)} %bitcast.61), channel_id=1, source_target_pairs={{0,16},{8,24},{16,0},{24,8},{1,17},{9,25},{17,1},{25,9},{2,18},{10... | collective-permute-start | bytes 4325384 | tf_op jit(solution)/shard_map/ppermute | solution.py:364
  230.7 34.2 %collective-permute-start.17 = (bf16[512,1408]{1,0:T(8,128)(2,1)S(1)}, bf16[512,1408]{1,0:T(8,128)(2,1)}, u32[]{:S(2)}, u32[]{:S(2)}) collective-permute-start(bf16[512,1408]{1,0:T(8,128)(2,1)S(1)} %bitcast.62), channel_id=1, source_target_pairs={{0,8},{8,0},{16,24},{24,16},{1,9},{9,1},{17,25},{25,17},{2,10},{10... | collective-permute-start | bytes 4325384 | tf_op jit(solution)/shard_map/ppermute | solution.py:364
  263.3 15.6 %collective-permute-start.20 = (bf16[256,1408]{1,0:T(8,128)(2,1)S(1)}, bf16[256,1408]{1,0:T(8,128)(2,1)S(1)}, u32[]{:S(2)}, u32[]{:S(2)}) collective-permute-start(bf16[256,1408]{1,0:T(8,128)(2,1)S(1)} %slice.366), channel_id=1, source_target_pairs={{0,8},{8,0},{16,24},{24,16},{1,9},{9,1},{17,25},{25,17},{2,10},{10... | collective-permute-start | bytes 2162696 | tf_op jit(solution)/shard_map/ppermute | solution.py:364
  266.0 15.3 %collective-permute-start.19 = (bf16[256,1408]{1,0:T(8,128)(2,1)S(1)}, bf16[256,1408]{1,0:T(8,128)(2,1)S(1)}, u32[]{:S(2)}, u32[]{:S(2)}) collective-permute-start(bf16[256,1408]{1,0:T(8,128)(2,1)S(1)} %slice.365), channel_id=1, source_target_pairs={{0,16},{8,24},{16,0},{24,8},{1,17},{9,25},{17,1},{25,9},{2,18},{10... | collective-permute-start | bytes 2162696 | tf_op jit(solution)/shard_map/ppermute | solution.py:364
  319.3 19.0 %collective-permute-start.21 = (bf16[256,1408]{1,0:T(8,128)(2,1)S(1)}, bf16[256,1408]{1,0:T(8,128)(2,1)S(1)}, u32[]{:S(2)}, u32[]{:S(2)}) collective-permute-start(bf16[256,1408]{1,0:T(8,128)(2,1)S(1)} %get-tuple-element.99), channel_id=1, source_target_pairs={{0,16},{8,24},{16,0},{24,8},{1,17},{9,25},{17,1},{25,9},{2,18},{10... | collective-permute-start | bytes 2162696 | tf_op jit(solution)/shard_map/ppermute | solution.py:364
  330.7 33.8 %collective-permute-start.24 = (bf16[512,1408]{1,0:T(8,128)(2,1)S(1)}, bf16[512,1408]{1,0:T(8,128)(2,1)S(1)}, u32[]{:S(2)}, u32[]{:S(2)}) collective-permute-start(bf16[512,1408]{1,0:T(8,128)(2,1)S(1)} %pad_maximum_fusion.3), channel_id=1, source_target_pairs={{0,16},{8,24},{16,0},{24,8},{1,17},{9,25},{17,1},{25,9},{2,18},{10... | collective-permute-start | bytes 4325384 | tf_op jit(solution)/shard_map/ppermute | solution.py:364
  338.6 25.9 %collective-permute-start.22 = (bf16[512,1408]{1,0:T(8,128)(2,1)S(1)}, bf16[512,1408]{1,0:T(8,128)(2,1)S(1)}, u32[]{:S(2)}, u32[]{:S(2)}) collective-permute-start(bf16[512,1408]{1,0:T(8,128)(2,1)S(1)} %pad_maximum_fusion.2), channel_id=1, source_target_pairs={{0,8},{8,0},{16,24},{24,16},{1,9},{9,1},{17,25},{25,17},{2,10},{10... | collective-permute-start | bytes 4325384 | tf_op jit(solution)/shard_map/ppermute | solution.py:364
  366.1 39.4 %all-to-all-start.2 = ((bf16[8,64,1408]{2,1,0:T(8,128)(2,1)}), bf16[8,64,1408]{2,1,0:T(8,128)(2,1)S(1)}, u32[]{:S(2)}, u32[]{:S(2)}) async-start(bf16[8,64,1408]{2,1,0:T(8,128)(2,1)} %bitcast.64), calls=%async_computation.3 | async-start | bytes 2883584 | tf_op jit(solution)/shard_map/all_to_all | solution.py:331
  370.5 84.1 %reduce-scatter.7.cloned.1.call-start = ((), (), s32[]{:S(2)}) async-start(), calls=%async_computation.12 | async-start | bytes 4718592 | tf_op jit(solution)/shard_map/reduce_scatter | solution.py:319
  378.7 15.4 %collective-permute-start.26 = (bf16[128,2176]{1,0:T(8,128)(2,1)}, bf16[128,2176]{1,0:T(8,128)(2,1)S(1)}, u32[]{:S(2)}, u32[]{:S(2)}) collective-permute-start(bf16[128,2176]{1,0:T(8,128)(2,1)} %after.23), channel_id=1, source_target_pairs={{0,16},{8,24},{16,0},{24,8},{1,17},{9,25},{17,1},{25,9},{2,18},{10... | collective-permute-start | bytes 1671176 | tf_op jit(solution)/shard_map/ppermute | solution.py:364
  406.6 108.7 %reduce-scatter.9.cloned.1.call-start = ((), (), s32[]{:S(2)}) async-start(), calls=%async_computation.13 | async-start | bytes 3932160 | tf_op jit(solution)/shard_map/reduce_scatter | solution.py:327
  456.7 102.2 %reduce-scatter.11.cloned.1.call-start = ((), (), s32[]{:S(2)}) async-start(), calls=%async_computation.14 | async-start | bytes 1310720 | tf_op jit(solution)/shard_map/reduce_scatter | solution.py:327
  467.1 32.3 %collective-permute-start.33 = (bf16[512,2048]{1,0:T(8,128)(2,1)}, bf16[512,2048]{1,0:T(8,128)(2,1)}, u32[]{:S(2)}, u32[]{:S(2)}) collective-permute-start(bf16[512,2048]{1,0:T(8,128)(2,1)} %slice.390), channel_id=1, source_target_pairs={{0,1},{1,0},{2,3},{3,2},{4,5},{5,4},{6,7},{7,6},{8,9},{9,8},{10,11... | collective-permute-start | bytes 6291464 | tf_op jit(solution)/shard_map/ppermute | solution.py:364
  479.0 36.4 %collective-permute-start.40 = (bf16[96,2048]{1,0:T(8,128)(2,1)}, bf16[96,2048]{1,0:T(8,128)(2,1)}, u32[]{:S(2)}, u32[]{:S(2)}) collective-permute-start(bf16[96,2048]{1,0:T(8,128)(2,1)} %get-tuple-element.83), channel_id=1, source_target_pairs={{0,8},{8,0},{16,24},{24,16},{1,9},{9,1},{17,25},{25,17},{2,10},{10... | collective-permute-start | bytes 1179656 | tf_op jit(solution)/shard_map/ppermute | solution.py:364
  481.2 16.7 %collective-permute-start.38 = (bf16[80,2048]{1,0:T(8,128)(2,1)S(1)}, bf16[80,2048]{1,0:T(8,128)(2,1)S(1)}, u32[]{:S(2)}, u32[]{:S(2)}) collective-permute-start(bf16[80,2048]{1,0:T(8,128)(2,1)S(1)} %get-tuple-element.84), channel_id=1, source_target_pairs={{0,16},{8,24},{16,0},{24,8},{1,17},{9,25},{17,1},{25,9},{2,18},{10... | collective-permute-start | bytes 983048 | tf_op jit(solution)/shard_map/ppermute | solution.py:364
  498.9 35.0 %collective-permute-start.39 = (bf16[176,2048]{1,0:T(8,128)(2,1)}, bf16[176,2048]{1,0:T(8,128)(2,1)}, u32[]{:S(2)}, u32[]{:S(2)}) collective-permute-start(bf16[176,2048]{1,0:T(8,128)(2,1)} %pad_maximum_fusion.5), channel_id=1, source_target_pairs={{0,8},{8,0},{16,24},{24,16},{1,9},{9,1},{17,25},{25,17},{2,10},{10... | collective-permute-start | bytes 2162696 | tf_op jit(solution)/shard_map/ppermute | solution.py:364
  504.2 18.7 %collective-permute-start.36 = (bf16[64,2048]{1,0:T(8,128)(2,1)}, bf16[64,2048]{1,0:T(8,128)(2,1)}, u32[]{:S(2)}, u32[]{:S(2)}) collective-permute-start(bf16[64,2048]{1,0:T(8,128)(2,1)} %get-tuple-element.95), channel_id=1, source_target_pairs={{0,8},{8,0},{16,24},{24,16},{1,9},{9,1},{17,25},{25,17},{2,10},{10... | collective-permute-start | bytes 786440 | tf_op jit(solution)/shard_map/ppermute | solution.py:364
  505.6 17.3 %collective-permute-start.34 = (bf16[64,2048]{1,0:T(8,128)(2,1)}, bf16[64,2048]{1,0:T(8,128)(2,1)}, u32[]{:S(2)}, u32[]{:S(2)}) collective-permute-start(bf16[64,2048]{1,0:T(8,128)(2,1)} %get-tuple-element.97), channel_id=1, source_target_pairs={{0,16},{8,24},{16,0},{24,8},{1,17},{9,25},{17,1},{25,9},{2,18},{10... | collective-permute-start | bytes 786440 | tf_op jit(solution)/shard_map/ppermute | solution.py:364
  518.5 19.4 %collective-permute-start.41 = (bf16[176,2048]{1,0:T(8,128)(2,1)}, bf16[176,2048]{1,0:T(8,128)(2,1)}, u32[]{:S(2)}, u32[]{:S(2)}) collective-permute-start(bf16[176,2048]{1,0:T(8,128)(2,1)} %pad_maximum_fusion.6), channel_id=1, source_target_pairs={{0,16},{8,24},{16,0},{24,8},{1,17},{9,25},{17,1},{25,9},{2,18},{10... | collective-permute-start | bytes 2162696 | tf_op jit(solution)/shard_map/ppermute | solution.py:364
  525.8 19.3 %collective-permute-start.35 = (bf16[128,2048]{1,0:T(8,128)(2,1)}, bf16[128,2048]{1,0:T(8,128)(2,1)}, u32[]{:S(2)}, u32[]{:S(2)}) collective-permute-start(bf16[128,2048]{1,0:T(8,128)(2,1)} %pad_maximum_fusion.10), channel_id=1, source_target_pairs={{0,8},{8,0},{16,24},{24,16},{1,9},{9,1},{17,25},{25,17},{2,10},{10... | collective-permute-start | bytes 1572872 | tf_op jit(solution)/shard_map/ppermute | solution.py:364
  526.3 33.5 %all-to-all-start.3 = ((bf16[8,64,768]{2,1,0:T(8,128)(2,1)}), bf16[8,64,768]{2,1,0:T(8,128)(2,1)}, u32[]{:S(2)}, u32[]{:S(2)}) async-start(bf16[8,64,768]{2,1,0:T(8,128)(2,1)} %bitcast.71), calls=%async_computation.6 | async-start | bytes 1572864 | tf_op jit(solution)/shard_map/all_to_all | solution.py:331
  531.9 24.1 %collective-permute-start.37 = (bf16[128,2048]{1,0:T(8,128)(2,1)S(1)}, bf16[128,2048]{1,0:T(8,128)(2,1)S(1)}, u32[]{:S(2)}, u32[]{:S(2)}) collective-permute-start(bf16[128,2048]{1,0:T(8,128)(2,1)S(1)} %pad_maximum_fusion.11), channel_id=1, source_target_pairs={{0,16},{8,24},{16,0},{24,8},{1,17},{9,25},{17,1},{25,9},{2,18},{10... | collective-permute-start | bytes 1572872 | tf_op jit(solution)/shard_map/ppermute | solution.py:364
  (94 other events, 619.0 us)
Sparse Core Ops, SparseCore 0:
  10.2 49.8 all-gather.3
  62.2 79.4 all-gather.5
  230.1 45.4 all-gather.7
  311.8 48.4 reduce-scatter.4
  406.7 47.7 reduce-scatter.6
  456.8 58.3 reduce-scatter.8
  518.1 27.1 reduce-scatter.10

commit v2 on v1

--- a/solution.py
+++ b/solution.py
@@ -576,15 +576,17 @@
     cotangent_low = (out_cotangent.astype(f32) * valid_here).astype(bf16)
 
     lead_own = swap(lead_blocks, PLANE)
+    expand_own = swap(after(expand_blocks, lead_own), SEQUENCE)
     input_low = jnp.concatenate([input_low, pad_columns(valid_here.astype(bf16))], axis=1)
     input_all, _ = gather_plane(after(input_low, lead_own))
     valid = input_all[:, depth : depth + 1].astype(f32)
     input_all = input_all[:, :depth]
     shrink = place_groups(gather_groups(after(shrink_weight.astype(bf16), valid)))
+    expand = place_groups(gather_groups(after(expand_own, shrink)))
     mixer_own = jnp.concatenate([lead_own, trail_low], axis=1)
-    cotangent_all = gather_tokens(cotangent_low)
-    mixer_near = gather_chips(after(mixer_own, cotangent_all))
-    mixer_near = after(mixer_near, expand_blocks, valid, shrink)
+    mixer_near = gather_chips(after(mixer_own, expand_own))
+    cotangent_all = gather_tokens(after(cotangent_low, mixer_near))
+    mixer_near = after(mixer_near, valid, expand)
     lead = mixer_near[:, : 3 * width]
     trail = mixer_near[:, 3 * width :].reshape(chips, 2 * nd, rows, width)
     trail = trail.transpose(0, 2, 1, 3).reshape(width, depth)
@@ -604,7 +606,6 @@
         gap,
     )
     carry = chain_chips(ends, False)
-    expand_own = swap(after(expand_blocks, carry), SEQUENCE)
     hidden, before, mix, squares = call_kernel(
         recur_mix_kernel,
         "recur_mix",
@@ -618,8 +619,7 @@
     )
     mixed_part = dot(mix, trail, ((1,), (0,))).astype(bf16)
     mixed_part = jnp.concatenate([mixed_part, pad_columns(split_low(squares))], axis=1)
-    mixed_sum = add_parts(scatter_plane(mixed_part, expand_own))
-    expand = place_groups(gather_groups(expand_own))
+    mixed_sum = add_parts(scatter_plane(mixed_part, cotangent_all))
     scale_two = lax.rsqrt(
         (mixed_sum[:, depth : depth + 1] + mixed_sum[:, depth + 1 : depth + 2]) / depth + norm_eps
     )
@@ -628,7 +628,7 @@
     scale_three = rms_scale(residual)
     normed_three = residual * scale_three
     feed_low = (normed_three * norm_gains[2]).astype(bf16)
-    feed_all = gather_tokens(feed_low)
+    feed_all = gather_tokens(after(feed_low, cotangent_all))
     expanded = dot(feed_all, expand, ((1,), (0,)))
     gate, up = expanded[:, :hid], expanded[:, hid:]
     gate_silu = jax.nn.silu(gate)

time: 625 us -> 625 us (level)
  waiting for transfers between devices: 275 us -> 263 us
  local copies, waits for them, and re-layouts: 61.4 us -> 69.7 us
  starting transfers between devices: 65.5 us -> 72.9 us
    all_gather x1, waiting for transfers between devices: 31.3 us -> 0.01 us  [gather_chips(): return lax.all_gather(part, 'z', axis=0, tiled=True)]
    all_gather x2, waiting for transfers between devices: 24.9 us -> 51.3 us  [gather_tokens(): return lax.all_gather(part, SEQUENCE, axis=0, tiled=True)]
    all_to_all x4, waiting for transfers between devices: 31.9 us -> 22.5 us  [swap(): return lax.all_to_all(blocks, axes, split_axis=0, concat_axis=0, tiled=True)]
    unnamed x145 -> x143, local copies, waits for them, and re-layouts: 30.9 us -> 37 us
  transfers between devices with their start and end apart: 58 -> 58, of which waited for: 36 -> 38; matrix products, arithmetic and copies ran while one was open for 22% -> 24% of each run, Pallas kernels for 3% -> 4%
where the time goes in v2:
time: 625 us; the launch traced here: 616 us
  waiting for transfers between devices  263 us (42%)
  other arithmetic  85.1 us (14%)
  matrix products  80.6 us (13%)
  starting transfers between devices  72.9 us (12%)
  local copies, waits for them, and re-layouts  69.7 us (11%)
  Pallas kernels  26.5 us (4%)
  between operations  17.7 us (3%)
    ppermute x41, waiting for transfers between devices, flip(): return lax.ppermute(part, axis, [(i, i ^ bit) for i in range(count)])  170 us
    dot_general x15, matrix products, dot(): lax.dot_general(left, right, (dims, ((), ())), preferred_element_type=f32)  80.6 us
    all_gather x2, waiting for transfers between devices, gather_tokens(): return lax.all_gather(part, SEQUENCE, axis=0, tiled=True)  51.3 us
    ppermute x41, starting transfers between devices, flip(): return lax.ppermute(part, axis, [(i, i ^ bit) for i in range(count)])  46.9 us
    unnamed x143, local copies, waits for them, and re-layouts  37 us
    reduce_sum x3, other arithmetic, squares_of(): return jnp.sum(matrices * matrices, axis=(0, 2))  27 us
    all_to_all x4, waiting for transfers between devices, swap(): return lax.all_to_all(blocks, axes, split_axis=0, concat_axis=0, tiled=True)  22.5 us
    all_to_all x4, starting transfers between devices, swap(): return lax.all_to_all(blocks, axes, split_axis=0, concat_axis=0, tiled=True)  18.6 us
  transfers between devices with their start and end apart: 58, of which 38 were waited for; matrix products, arithmetic and copies ran while one was open for 24% of the time, Pallas kernels for 4%

profile of v2, /device:TPU:0, one launch (start us, length us, event | category | flops | bytes accessed | tf_op | source)
XLA Modules:
  0.0 615.7 jit_solution(8971054318123605724)
XLA Ops:
  10.3 5.2 all-to-all-start
  22.3 6.0 all-to-all-done
  31.5 5.4 all-to-all-start.1
  57.0 14.9 %all-to-all-done.1 = bf16[8,64,1408]{2,1,0:T(8,128)(2,1)S(1)} async-done(((bf16[8,64,1408]{2,1,0:T(8,128)(2,1)}), bf16[8,64,1408]{2,1,0:T(8,128)(2,1)S(1)}, u32[]{:S(2)}, u32[]{:S(2)}) %all-to-all-start.1) | async-done | bytes 1441824 | tf_op jit(solution)/shard_map/all_to_all | solution.py:331
  84.4 13.8 %collective-permute-done.6 = bf16[176,2048]{1,0:T(8,128)(2,1)} collective-permute-done((bf16[176,2048]{1,0:T(8,128)(2,1)}, bf16[176,2048]{1,0:T(8,128)(2,1)}, u32[]{:S(2)}, u32[]{:S(2)}) %collective-permute-start.6) | collective-permute-done | bytes 720928 | tf_op jit(solution)/shard_map/ppermute | solution.py:364
  116.2 28.1 %collective-permute-done.10 = bf16[512,1408]{1,0:T(8,128)(2,1)S(1)} collective-permute-done((bf16[512,1408]{1,0:T(8,128)(2,1)}, bf16[512,1408]{1,0:T(8,128)(2,1)S(1)}, u32[]{:S(2)}, u32[]{:S(2)}) %collective-permute-start.10) | collective-permute-done | bytes 1441824 | tf_op jit(solution)/shard_map/ppermute | solution.py:364
  153.9 7.1 %collective-permute-done.12 = bf16[256,1408]{1,0:T(8,128)(2,1)S(1)} collective-permute-done((bf16[256,1408]{1,0:T(8,128)(2,1)S(1)}, bf16[256,1408]{1,0:T(8,128)(2,1)S(1)}, u32[]{:S(2)}, u32[]{:S(2)}) %collective-permute-start.12) | collective-permute-done | bytes 720928 | tf_op jit(solution)/shard_map/ppermute | solution.py:364
  162.3 6.2 %fusion.3.logits_ref = f32[1024,768]{1,0:T(8,128)S(1)} fusion(bf16[1024,2176]{1,0:T(8,128)(2,1)} %constant_dynamic-update-slice_fusion.5, bf16[2048,1024]{1,0:T(8,128)(2,1)} %after.24), kind=kOutput, calls=%fused_computation.14 | convolution fusion | flops 3221225472 | bytes 10485760 | tf_op jit(solution)/shard_map/dot_general | solution.py:529
  194.8 6.4 %collective-permute-done.17 = bf16[64,2176]{1,0:T(8,128)(2,1)S(1)} collective-permute-done((bf16[64,2176]{1,0:T(8,128)(2,1)S(1)}, bf16[64,2176]{1,0:T(8,128)(2,1)S(1)}, u32[]{:S(2)}, u32[]{:S(2)}) %collective-permute-start.17) | collective-permute-done | bytes 278560 | tf_op jit(solution)/shard_map/ppermute | solution.py:364
  203.5 6.2 all-gather.6.cloned.1.call-done.refs_1_.refs_0_
  212.7 12.0 %collective-permute-done.20 = bf16[128,2176]{1,0:T(8,128)(2,1)S(1)} collective-permute-done((bf16[128,2176]{1,0:T(8,128)(2,1)}, bf16[128,2176]{1,0:T(8,128)(2,1)S(1)}, u32[]{:S(2)}, u32[]{:S(2)}) %collective-permute-start.20) | collective-permute-done | bytes 557088 | tf_op jit(solution)/shard_map/ppermute | solution.py:364
  231.5 45.2 %all-gather.8.cloned.1.call-done = bf16[1024,2048]{1,0:T(8,128)(2,1)} async-done(((bf16[128,2048]{1,0:T(8,128)(2,1)}), bf16[1024,2048]{1,0:T(8,128)(2,1)}) %all-gather.8.cloned.1.call-update) | async-done | bytes 4194320 | tf_op jit(solution)/shard_map/all_gather | solution.py:315
  276.7 10.6 %fusion.86 = f32[1024,1408]{1,0:T(8,128)S(1)} fusion(bf16[1024,2048]{1,0:T(8,128)(2,1)} %all-gather.8.cloned.1.call-done, bf16[2048,1408]{1,0:T(8,128)(2,1)} %maximum_dynamic-update-slice_fusion.refs_2_), kind=kOutput, calls=%fused_computation.224 | convolution fusion | flops 5905580032 | bytes 15728640 | tf_op jit(solution)/shard_map/dot_general | solution.py:529
  287.3 5.4 multiply_convert_fusion.1
  294.4 11.3 %convolution_convert_fusion = bf16[1024,2048]{1,0:T(8,128)(2,1)} fusion(bf16[2048,1408]{1,0:T(8,128)(2,1)} %maximum_dynamic-update-slice_fusion.refs_2_, bf16[1024,704]{1,0:T(8,128)(2,1)S(1)} %get-tuple-element.79, bf16[1024,704]{1,0:T(8,128)(2,1)S(1)} %get-tuple-element.78), kind=kOutput, calls=%fused_computation.8 | convolution fusion | flops 5913444352 | bytes 12845056 | tf_op jit(solution)/shard_map/dot_general | solution.py:529
  317.1 11.4 %collective-permute-done.23 = bf16[256,1408]{1,0:T(8,128)(2,1)S(1)} collective-permute-done((bf16[256,1408]{1,0:T(8,128)(2,1)S(1)}, bf16[256,1408]{1,0:T(8,128)(2,1)S(1)}, u32[]{:S(2)}, u32[]{:S(2)}) %collective-permute-start.23) | collective-permute-done | bytes 720928 | tf_op jit(solution)/shard_map/ppermute | solution.py:364
  336.4 26.4 %collective-permute-done.24 = bf16[512,1408]{1,0:T(8,128)(2,1)S(1)} collective-permute-done((bf16[512,1408]{1,0:T(8,128)(2,1)S(1)}, bf16[512,1408]{1,0:T(8,128)(2,1)S(1)}, u32[]{:S(2)}, u32[]{:S(2)}) %collective-permute-start.24) | collective-permute-done | bytes 1441824 | tf_op jit(solution)/shard_map/ppermute | solution.py:364
  381.2 7.8 %convolution_convert_fusion.1.refs_0_ = bf16[1024,2048]{1,0:T(8,128)(2,1)} fusion(bf16[1024,704]{1,0:T(8,128)(2,1)} %get-tuple-element.80, bf16[704,2048]{1,0:T(8,128)(2,1)} %copy-done.38), kind=kOutput, calls=%fused_computation.9 | convolution fusion | flops 2954887168 | bytes 8519680 | tf_op jit(solution)/shard_map/dot_general | solution.py:529
  406.5 4.7 collective-permute-done.29
  413.4 4.5 fusion.73.grad_mix_ref
  418.0 6.1 recur_reverse.1
  426.9 4.5 convolution_convert_fusion.9.refs_0_
  440.3 8.0 %fusion.5.refs_0_ = bf16[2048,768]{1,0:T(8,128)(2,1)} fusion(bf16[1024,768]{1,0:T(8,128)(2,1)S(1)} %recur_finish.1.refs_0_, bf16[1024,2176]{1,0:T(8,128)(2,1)} %constant_dynamic-update-slice_fusion.5), kind=kOutput, calls=%fused_computation.16 | convolution fusion | flops 3222798336 | bytes 8912896 | tf_op jit(solution)/shard_map/dot_general | solution.py:529
  448.4 7.7 %reduce-scatter.7.cloned.1.call-done = bf16[128,2048]{1,0:T(8,128)(2,1)} async-done(((bf16[1024,2048]{1,0:T(8,128)(2,1)}), bf16[128,2048]{1,0:T(8,128)(2,1)}) %reduce-scatter.7.cloned.1.call-update) | async-done | bytes 524304 | tf_op jit(solution)/shard_map/reduce_scatter | solution.py:319
  459.6 5.6 convolution_convert_fusion.3.refs_1_
  474.1 5.6 convolution_convert_fusion.4
  484.2 12.9 %multiply_reduce_fusion = (f32[2]{0:T(128)S(1)}, f32[64,2,5632]{2,1,0:T(2,128)}, f32[64,2,5632]{2,1,0:T(2,128)}, f32[64,2,5632]{2,1,0:T(2,128)}, f32[2]{0:T(128)S(1)}) fusion(f32[64,2,5632]{2,1,0:T(2,128)S(1)} %copy-done.2, f32[64,2,5632]{2,1,0:T(2,128)S(1)} %copy-done.36, f32[64,2,5632]{2,1,0:T(2,128)S(1)} %copy-done.51, f32[64,2,5632]{2,1,0:T(2,128)S(1)} %copy-done.52), kind=kLoop, calls=%fused_computation.32 | loop fusion | flops 12255228 | bytes 20185104 | tf_op jit(solution)/shard_map/reduce_sum | solution.py:44
  507.7 9.1 %reduce-scatter.9.cloned.1.call-done.refs_1_ = bf16[512,768]{1,0:T(8,128)(2,1)} async-done(((bf16[2048,768]{1,0:T(8,128)(2,1)}), bf16[512,768]{1,0:T(8,128)(2,1)}) %reduce-scatter.9.cloned.1.call-update) | async-done | bytes 786448 | tf_op jit(solution)/shard_map/reduce_scatter | solution.py:327
  539.3 6.2 multiply_reduce_fusion.4
  546.6 11.0 %collective-permute-done.37.refs_2_ = bf16[128,2048]{1,0:T(8,128)(2,1)S(1)} collective-permute-done((bf16[128,2048]{1,0:T(8,128)(2,1)S(1)}, bf16[128,2048]{1,0:T(8,128)(2,1)S(1)}, u32[]{:S(2)}, u32[]{:S(2)}) %collective-permute-start.37) | collective-permute-done | bytes 524320 | tf_op jit(solution)/shard_map/ppermute | solution.py:364
  564.7 7.9 %multiply_reduce_fusion.2 = (f32[4]{0:T(128)S(1)}, f32[64,4,2048]{2,1,0:T(4,128)}, f32[64,4,2048]{2,1,0:T(4,128)}, f32[64,4,2048]{2,1,0:T(4,128)}, f32[4]{0:T(128)S(1)}) fusion(f32[64,4,2048]{2,1,0:T(4,128)S(1)} %copy-done.8, f32[64,4,2048]{2,1,0:T(4,128)} %join_columns.2, f32[64,4,2048]{2,1,0:T(4,128)} %param.25, f32[64,4,2048]{2,1,0:T(4,128)} %param.24), kind=kLoop, calls=%fused_computation.45 | loop fusion | flops 8912888 | bytes 14680096 | tf_op jit(solution)/shard_map/reduce_sum | solution.py:44
  596.1 5.0 multiply_subtract_fusion.1
  (401 shorter events, 270.1 us)
Async XLA Ops:
  10.3 17.9 %all-to-all-start = ((bf16[8,64,768]{2,1,0:T(8,128)(2,1)}), bf16[8,64,768]{2,1,0:T(8,128)(2,1)}, u32[]{:S(2)}, u32[]{:S(2)}) async-start(bf16[8,64,768]{2,1,0:T(8,128)(2,1)} %bitcast.4), calls=%async_computation | async-start | bytes 1572864 | tf_op jit(solution)/shard_map/all_to_all | solution.py:331
  31.5 40.4 %all-to-all-start.1 = ((bf16[8,64,1408]{2,1,0:T(8,128)(2,1)}), bf16[8,64,1408]{2,1,0:T(8,128)(2,1)S(1)}, u32[]{:S(2)}, u32[]{:S(2)}) async-start(bf16[8,64,1408]{2,1,0:T(8,128)(2,1)} %bitcast.58), calls=%async_computation.1 | async-start | bytes 2883584 | tf_op jit(solution)/shard_map/all_to_all | solution.py:331
  36.9 125.3 %all-gather.4.cloned.1.call-start = ((), (), s32[]{:S(2)}) async-start(), calls=%async_computation.8 | async-start | bytes 5242880 | tf_op jit(solution)/shard_map/all_gather | solution.py:323
  54.7 20.6 %collective-permute-start.4 = (bf16[512,2176]{1,0:T(8,128)(2,1)}, bf16[512,2176]{1,0:T(8,128)(2,1)}, u32[]{:S(2)}, u32[]{:S(2)}) collective-permute-start(bf16[512,2176]{1,0:T(8,128)(2,1)} %get-tuple-element.114), channel_id=1, source_target_pairs={{0,1},{1,0},{2,3},{3,2},{4,5},{5,4},{6,7},{7,6},{8,9},{9,8},{10,11... | collective-permute-start | bytes 6684680 | tf_op jit(solution)/shard_map/ppermute | solution.py:364
  73.0 136.6 %all-gather.6.cloned.1.call-start = ((), (), s32[]{:S(2)}) async-start(), calls=%async_computation.9 | async-start | bytes 4718592 | tf_op jit(solution)/shard_map/all_gather | solution.py:315
  80.3 18.0 %collective-permute-start.6 = (bf16[176,2048]{1,0:T(8,128)(2,1)}, bf16[176,2048]{1,0:T(8,128)(2,1)}, u32[]{:S(2)}, u32[]{:S(2)}) collective-permute-start(bf16[176,2048]{1,0:T(8,128)(2,1)} %after.22), channel_id=1, source_target_pairs={{0,16},{8,24},{16,0},{24,8},{1,17},{9,25},{17,1},{25,9},{2,18},{10... | collective-permute-start | bytes 2162696 | tf_op jit(solution)/shard_map/ppermute | solution.py:364
  81.7 19.1 %collective-permute-start.5 = (bf16[176,2048]{1,0:T(8,128)(2,1)}, bf16[176,2048]{1,0:T(8,128)(2,1)}, u32[]{:S(2)}, u32[]{:S(2)}) collective-permute-start(bf16[176,2048]{1,0:T(8,128)(2,1)} %after.22), channel_id=1, source_target_pairs={{0,8},{8,0},{16,24},{24,16},{1,9},{9,1},{17,25},{25,17},{2,10},{10... | collective-permute-start | bytes 2162696 | tf_op jit(solution)/shard_map/ppermute | solution.py:364
  113.0 31.3 %collective-permute-start.10 = (bf16[512,1408]{1,0:T(8,128)(2,1)}, bf16[512,1408]{1,0:T(8,128)(2,1)S(1)}, u32[]{:S(2)}, u32[]{:S(2)}) collective-permute-start(bf16[512,1408]{1,0:T(8,128)(2,1)} %after.23), channel_id=1, source_target_pairs={{0,16},{8,24},{16,0},{24,8},{1,17},{9,25},{17,1},{25,9},{2,18},{10... | collective-permute-start | bytes 4325384 | tf_op jit(solution)/shard_map/ppermute | solution.py:364
  114.5 32.7 %collective-permute-start.9 = (bf16[512,1408]{1,0:T(8,128)(2,1)}, bf16[512,1408]{1,0:T(8,128)(2,1)S(1)}, u32[]{:S(2)}, u32[]{:S(2)}) collective-permute-start(bf16[512,1408]{1,0:T(8,128)(2,1)} %after.23), channel_id=1, source_target_pairs={{0,8},{8,0},{16,24},{24,16},{1,9},{9,1},{17,25},{25,17},{2,10},{10... | collective-permute-start | bytes 4325384 | tf_op jit(solution)/shard_map/ppermute | solution.py:364
  144.4 16.6 %collective-permute-start.12 = (bf16[256,1408]{1,0:T(8,128)(2,1)S(1)}, bf16[256,1408]{1,0:T(8,128)(2,1)S(1)}, u32[]{:S(2)}, u32[]{:S(2)}) collective-permute-start(bf16[256,1408]{1,0:T(8,128)(2,1)S(1)} %slice.346), channel_id=1, source_target_pairs={{0,8},{8,0},{16,24},{24,16},{1,9},{9,1},{17,25},{25,17},{2,10},{10... | collective-permute-start | bytes 2162696 | tf_op jit(solution)/shard_map/ppermute | solution.py:364
  162.3 114.5 %all-gather.8.cloned.1.call-start = ((), (), s32[]{:S(2)}) async-start(), calls=%async_computation.10 | async-start | bytes 4718592 | tf_op jit(solution)/shard_map/all_gather | solution.py:315
  231.5 139.0 %reduce-scatter.5.cloned.1.call-start = ((), (), s32[]{:S(2)}) async-start(), calls=%async_computation.11 | async-start | bytes 4718592 | tf_op jit(solution)/shard_map/reduce_scatter | solution.py:319
  310.1 18.3 %collective-permute-start.23 = (bf16[256,1408]{1,0:T(8,128)(2,1)S(1)}, bf16[256,1408]{1,0:T(8,128)(2,1)S(1)}, u32[]{:S(2)}, u32[]{:S(2)}) collective-permute-start(bf16[256,1408]{1,0:T(8,128)(2,1)S(1)} %get-tuple-element.100), channel_id=1, source_target_pairs={{0,8},{8,0},{16,24},{24,16},{1,9},{9,1},{17,25},{25,17},{2,10},{10... | collective-permute-start | bytes 2162696 | tf_op jit(solution)/shard_map/ppermute | solution.py:364
  313.6 19.0 %collective-permute-start.21 = (bf16[256,1408]{1,0:T(8,128)(2,1)S(1)}, bf16[256,1408]{1,0:T(8,128)(2,1)S(1)}, u32[]{:S(2)}, u32[]{:S(2)}) collective-permute-start(bf16[256,1408]{1,0:T(8,128)(2,1)S(1)} %get-tuple-element.99), channel_id=1, source_target_pairs={{0,16},{8,24},{16,0},{24,8},{1,17},{9,25},{17,1},{25,9},{2,18},{10... | collective-permute-start | bytes 2162696 | tf_op jit(solution)/shard_map/ppermute | solution.py:364
  328.8 34.0 %collective-permute-start.24 = (bf16[512,1408]{1,0:T(8,128)(2,1)S(1)}, bf16[512,1408]{1,0:T(8,128)(2,1)S(1)}, u32[]{:S(2)}, u32[]{:S(2)}) collective-permute-start(bf16[512,1408]{1,0:T(8,128)(2,1)S(1)} %pad_maximum_fusion.3), channel_id=1, source_target_pairs={{0,16},{8,24},{16,0},{24,8},{1,17},{9,25},{17,1},{25,9},{2,18},{10... | collective-permute-start | bytes 4325384 | tf_op jit(solution)/shard_map/ppermute | solution.py:364
  332.9 32.2 %collective-permute-start.22 = (bf16[512,1408]{1,0:T(8,128)(2,1)S(1)}, bf16[512,1408]{1,0:T(8,128)(2,1)S(1)}, u32[]{:S(2)}, u32[]{:S(2)}) collective-permute-start(bf16[512,1408]{1,0:T(8,128)(2,1)S(1)} %pad_maximum_fusion.2), channel_id=1, source_target_pairs={{0,8},{8,0},{16,24},{24,16},{1,9},{9,1},{17,25},{25,17},{2,10},{10... | collective-permute-start | bytes 4325384 | tf_op jit(solution)/shard_map/ppermute | solution.py:364
  366.7 38.5 %all-to-all-start.2 = ((bf16[8,64,1408]{2,1,0:T(8,128)(2,1)}), bf16[8,64,1408]{2,1,0:T(8,128)(2,1)S(1)}, u32[]{:S(2)}, u32[]{:S(2)}) async-start(bf16[8,64,1408]{2,1,0:T(8,128)(2,1)} %bitcast.61), calls=%async_computation.3 | async-start | bytes 2883584 | tf_op jit(solution)/shard_map/all_to_all | solution.py:331
  370.2 85.8 %reduce-scatter.7.cloned.1.call-start = ((), (), s32[]{:S(2)}) async-start(), calls=%async_computation.12 | async-start | bytes 4718592 | tf_op jit(solution)/shard_map/reduce_scatter | solution.py:319
  378.0 15.1 %collective-permute-start.25 = (bf16[128,2176]{1,0:T(8,128)(2,1)}, bf16[128,2176]{1,0:T(8,128)(2,1)S(1)}, u32[]{:S(2)}, u32[]{:S(2)}) collective-permute-start(bf16[128,2176]{1,0:T(8,128)(2,1)} %after.29), channel_id=1, source_target_pairs={{0,8},{8,0},{16,24},{24,16},{1,9},{9,1},{17,25},{25,17},{2,10},{10... | collective-permute-start | bytes 1671176 | tf_op jit(solution)/shard_map/ppermute | solution.py:364
  379.7 15.2 %collective-permute-start.26 = (bf16[128,2176]{1,0:T(8,128)(2,1)}, bf16[128,2176]{1,0:T(8,128)(2,1)S(1)}, u32[]{:S(2)}, u32[]{:S(2)}) collective-permute-start(bf16[128,2176]{1,0:T(8,128)(2,1)} %after.29), channel_id=1, source_target_pairs={{0,16},{8,24},{16,0},{24,8},{1,17},{9,25},{17,1},{25,9},{2,18},{10... | collective-permute-start | bytes 1671176 | tf_op jit(solution)/shard_map/ppermute | solution.py:364
  406.3 110.5 %reduce-scatter.9.cloned.1.call-start = ((), (), s32[]{:S(2)}) async-start(), calls=%async_computation.13 | async-start | bytes 3932160 | tf_op jit(solution)/shard_map/reduce_scatter | solution.py:327
  458.2 102.1 %reduce-scatter.11.cloned.1.call-start = ((), (), s32[]{:S(2)}) async-start(), calls=%async_computation.14 | async-start | bytes 1310720 | tf_op jit(solution)/shard_map/reduce_scatter | solution.py:327
  468.7 32.3 %collective-permute-start.33 = (bf16[512,2048]{1,0:T(8,128)(2,1)}, bf16[512,2048]{1,0:T(8,128)(2,1)}, u32[]{:S(2)}, u32[]{:S(2)}) collective-permute-start(bf16[512,2048]{1,0:T(8,128)(2,1)} %slice.390), channel_id=1, source_target_pairs={{0,1},{1,0},{2,3},{3,2},{4,5},{5,4},{6,7},{7,6},{8,9},{9,8},{10,11... | collective-permute-start | bytes 6291464 | tf_op jit(solution)/shard_map/ppermute | solution.py:364
  480.5 36.3 %collective-permute-start.40 = (bf16[96,2048]{1,0:T(8,128)(2,1)}, bf16[96,2048]{1,0:T(8,128)(2,1)}, u32[]{:S(2)}, u32[]{:S(2)}) collective-permute-start(bf16[96,2048]{1,0:T(8,128)(2,1)} %get-tuple-element.83), channel_id=1, source_target_pairs={{0,8},{8,0},{16,24},{24,16},{1,9},{9,1},{17,25},{25,17},{2,10},{10... | collective-permute-start | bytes 1179656 | tf_op jit(solution)/shard_map/ppermute | solution.py:364
  482.7 16.7 %collective-permute-start.38 = (bf16[80,2048]{1,0:T(8,128)(2,1)S(1)}, bf16[80,2048]{1,0:T(8,128)(2,1)S(1)}, u32[]{:S(2)}, u32[]{:S(2)}) collective-permute-start(bf16[80,2048]{1,0:T(8,128)(2,1)S(1)} %get-tuple-element.84), channel_id=1, source_target_pairs={{0,16},{8,24},{16,0},{24,8},{1,17},{9,25},{17,1},{25,9},{2,18},{10... | collective-permute-start | bytes 983048 | tf_op jit(solution)/shard_map/ppermute | solution.py:364
  500.4 35.0 %collective-permute-start.39 = (bf16[176,2048]{1,0:T(8,128)(2,1)}, bf16[176,2048]{1,0:T(8,128)(2,1)}, u32[]{:S(2)}, u32[]{:S(2)}) collective-permute-start(bf16[176,2048]{1,0:T(8,128)(2,1)} %pad_maximum_fusion.5), channel_id=1, source_target_pairs={{0,8},{8,0},{16,24},{24,16},{1,9},{9,1},{17,25},{25,17},{2,10},{10... | collective-permute-start | bytes 2162696 | tf_op jit(solution)/shard_map/ppermute | solution.py:364
  505.7 18.7 %collective-permute-start.36 = (bf16[64,2048]{1,0:T(8,128)(2,1)}, bf16[64,2048]{1,0:T(8,128)(2,1)}, u32[]{:S(2)}, u32[]{:S(2)}) collective-permute-start(bf16[64,2048]{1,0:T(8,128)(2,1)} %get-tuple-element.95), channel_id=1, source_target_pairs={{0,8},{8,0},{16,24},{24,16},{1,9},{9,1},{17,25},{25,17},{2,10},{10... | collective-permute-start | bytes 786440 | tf_op jit(solution)/shard_map/ppermute | solution.py:364
  507.1 17.3 %collective-permute-start.34 = (bf16[64,2048]{1,0:T(8,128)(2,1)}, bf16[64,2048]{1,0:T(8,128)(2,1)}, u32[]{:S(2)}, u32[]{:S(2)}) collective-permute-start(bf16[64,2048]{1,0:T(8,128)(2,1)} %get-tuple-element.97), channel_id=1, source_target_pairs={{0,16},{8,24},{16,0},{24,8},{1,17},{9,25},{17,1},{25,9},{2,18},{10... | collective-permute-start | bytes 786440 | tf_op jit(solution)/shard_map/ppermute | solution.py:364
  520.0 19.4 %collective-permute-start.41 = (bf16[176,2048]{1,0:T(8,128)(2,1)}, bf16[176,2048]{1,0:T(8,128)(2,1)}, u32[]{:S(2)}, u32[]{:S(2)}) collective-permute-start(bf16[176,2048]{1,0:T(8,128)(2,1)} %pad_maximum_fusion.6), channel_id=1, source_target_pairs={{0,16},{8,24},{16,0},{24,8},{1,17},{9,25},{17,1},{25,9},{2,18},{10... | collective-permute-start | bytes 2162696 | tf_op jit(solution)/shard_map/ppermute | solution.py:364
  527.3 19.3 %collective-permute-start.35 = (bf16[128,2048]{1,0:T(8,128)(2,1)}, bf16[128,2048]{1,0:T(8,128)(2,1)}, u32[]{:S(2)}, u32[]{:S(2)}) collective-permute-start(bf16[128,2048]{1,0:T(8,128)(2,1)} %pad_maximum_fusion.10), channel_id=1, source_target_pairs={{0,8},{8,0},{16,24},{24,16},{1,9},{9,1},{17,25},{25,17},{2,10},{10... | collective-permute-start | bytes 1572872 | tf_op jit(solution)/shard_map/ppermute | solution.py:364
  527.9 33.5 %all-to-all-start.3 = ((bf16[8,64,768]{2,1,0:T(8,128)(2,1)}), bf16[8,64,768]{2,1,0:T(8,128)(2,1)}, u32[]{:S(2)}, u32[]{:S(2)}) async-start(bf16[8,64,768]{2,1,0:T(8,128)(2,1)} %bitcast.66), calls=%async_computation.6 | async-start | bytes 1572864 | tf_op jit(solution)/shard_map/all_to_all | solution.py:331
  533.4 24.1 %collective-permute-start.37 = (bf16[128,2048]{1,0:T(8,128)(2,1)S(1)}, bf16[128,2048]{1,0:T(8,128)(2,1)S(1)}, u32[]{:S(2)}, u32[]{:S(2)}) collective-permute-start(bf16[128,2048]{1,0:T(8,128)(2,1)S(1)} %pad_maximum_fusion.11), channel_id=1, source_target_pairs={{0,16},{8,24},{16,0},{24,8},{1,17},{9,25},{17,1},{25,9},{2,18},{10... | collective-permute-start | bytes 1572872 | tf_op jit(solution)/shard_map/ppermute | solution.py:364
  (93 other events, 572.1 us)
Sparse Core Ops, SparseCore 0:
  73.2 79.5 all-gather.3
  162.4 47.2 all-gather.5
  231.6 45.0 all-gather.7
  305.9 48.7 reduce-scatter.4
  406.4 49.6 reduce-scatter.6
  458.4 58.3 reduce-scatter.8
  519.6 27.1 reduce-scatter.10
